TPU v7x, 256 devices: a whole 4x4x8 slice. The times are simulated.
256 devices in a mesh: dp: 16 (over z, core), tensor: 16 (over y, x).
Axes of the slice: x: 4, y: 4, z: 8, core: 2. Of those that a mesh axis runs over, the one named last changes fastest.
Arguments:
- inputs: bfloat16 [2048, 6144], P('dp'), may hold values from -16 to 16
- preact: bfloat16 [2048, 24576], P('dp', 'tensor'), may hold values from -8 to 8
- grad_act: bfloat16 [2048, 24576], P('dp', 'tensor'), may hold values from -80 to 80
- weight: bfloat16 [6144, 24576], P('dp', 'tensor'), may hold values from -0.078125 to 0.078125
Outputs:
- grad_input: bfloat16 [2048, 6144], P('dp')
- weight_grad: float32 [6144, 24576], P('dp', 'tensor')
- grad_amax: float32 [], replicated
All inputs are finite; a program needn't handle non-finite values.
Results may differ from a plain program's by a relative error of at most 0.02.
Values may be sent and summed in bfloat16 or wider, within the bound.
No kernel may reach another device: no remote copies, remote signals or barrier semaphores. Data moves between devices by JAX's collectives and lax.ppermute only.
A program may use at most 192 MiB of HBM per device.

v0:
```python
import math

import jax
import jax.numpy as jnp
from jax import lax
from jax.sharding import PartitionSpec as P

gelu_coeff = math.sqrt(2.0 / math.pi)
epsilon = 1e-06


def slope_of(preact):
    values = preact.astype(jnp.float32)
    inner_arg = gelu_coeff * (values + 0.044715 * values * values * values)
    tanh_val = jnp.tanh(inner_arg)
    return 0.5 * (1.0 + tanh_val) + 0.5 * values * (1.0 - tanh_val * tanh_val) * gelu_coeff * (
        1.0 + 3.0 * 0.044715 * values * values
    )


def to_wire(values):
    return lax.optimization_barrier(values.astype(jnp.bfloat16)).astype(jnp.float32)


def shared_max(local_max):
    return lax.pmax(local_max, ("dp", "tensor"))


def outer_rows(left, right):
    return lax.dot_general(
        left, right, (((0,), (0,)), ((), ())), preferred_element_type=jnp.float32
    )


def on_device(inputs, preact, grad_act, weight):
    grad_pre = (grad_act.astype(jnp.float32) * slope_of(preact)).astype(jnp.bfloat16)
    all_pre = lax.all_gather(grad_pre, "dp", axis=0, tiled=True)
    block_part = lax.dot_general(
        all_pre, weight, (((1,), (1,)), ((), ())), preferred_element_type=jnp.float32
    )
    block_part = to_wire(block_part)
    summed = lax.psum(block_part.astype(jnp.bfloat16), "tensor")
    grad_input = lax.all_to_all(summed, "dp", split_axis=0, concat_axis=1, tiled=True)
    partial_grad = outer_rows(inputs, grad_pre)
    grad_amax = shared_max(jnp.max(jnp.abs(partial_grad)))
    grad_scale = 1.0 / (grad_amax + epsilon)
    weight_grad = lax.psum_scatter(
        (partial_grad * grad_scale).astype(jnp.bfloat16), "dp", scatter_dimension=0, tiled=True
    ).astype(jnp.float32)
    return (grad_input, weight_grad, grad_amax)


def solution(mesh):
    placed = (P("dp", None), P("dp", "tensor"), P("dp", "tensor"), P("dp", "tensor"))
    return jax.shard_map(
        on_device,
        mesh=mesh,
        in_specs=placed,
        out_specs=(P("dp", None), P("dp", "tensor"), P()),
        check_vma=False,
    )
```

profile of v0, /device:TPU:32, one launch (start us, length us, event | category | flops | bytes accessed | tf_op | source)
XLA Modules:
  0.0 359.2 jit_solution(8793022645366510722)
XLA Ops:
  7.2 0.0 copy-start
  7.2 0.0 all-gather.2.cloned.1.call-start
  7.2 2.5 fusion.8
  9.7 0.0 all-gather.2.cloned.1.call-update
  9.8 0.0 copy-start.2
  9.8 0.0 all-reduce.2.cloned.1.call-start
  9.8 0.0 copy-done
  9.8 16.8 %abs_reduce_fusion = (f32[]{:T(128)}, f32[1536,6144]{1,0:T(8,128)}) fusion(bf16[128,1536]{1,0:T(8,128)(2,1)} %fusion.8, bf16[128,6144]{1,0:T(8,128)(2,1)S(1)} %copy-done), kind=kOutput, calls=%fused_computation.1 | convolution fusion | flops 2434793472 | bytes 39714820 | tf_op jit(solution)/shard_map/dot_general | solution.py:30
  26.7 80.6 %pmax.7 = f32[]{:T(128)} all-reduce(f32[]{:T(128)} %get-tuple-element.9), channel_id=1, replica_groups=mesh['dp'=16,'tensor'=16] {'dp','tensor'}, use_global_device_ids=true, to_apply=%region_2.0 | all-reduce | flops 1 | bytes 8 | tf_op jit(solution)/shard_map/pmax | solution.py:26
  108.0 0.0 all-gather.2.cloned.1.call-done
  108.0 0.0 copy-done.2
  108.0 7.4 %convolution_convert_fusion = bf16[2048,384]{1,0:T(8,128)(2,1)} fusion(bf16[2048,1536]{1,0:T(8,128)(2,1)} %all-gather.2.cloned.1.call-done, bf16[384,1536]{1,0:T(8,128)(2,1)S(1)} %copy-done.2), kind=kOutput, calls=%fused_computation.3 | convolution fusion | flops 2416705536 | bytes 9043968 | tf_op jit(solution)/shard_map/dot_general | solution.py:38
  115.4 0.0 all-reduce.2.cloned.1.call-update
  115.4 0.0 reduce-scatter.4.cloned.1.call-start
  115.5 21.5 %fusion = bf16[6144,1536]{0,1:T(8,128)(2,1)} fusion(f32[1536,6144]{1,0:T(8,128)} %get-tuple-element.10, f32[]{:T(128)S(6)} %div.3), kind=kLoop, calls=%fused_computation.2 | loop fusion | flops 18874368 | bytes 56623108 | tf_op jit(solution)/shard_map/convert_element_type | solution.py:48
  136.9 24.7 %copy.11 = bf16[6144,1536]{1,0:T(8,128)(2,1)} copy(bf16[6144,1536]{0,1:T(8,128)(2,1)} %fusion) | data formatting | bytes 37748736
  161.6 0.0 reduce-scatter.4.cloned.1.call-update
  161.6 48.3 %all-reduce.2.cloned.1.call-done = bf16[16,128,384]{2,1,0:T(8,128)(2,1)} async-done(((bf16[16,128,384]{2,1,0:T(8,128)(2,1)}), bf16[16,128,384]{2,1,0:T(8,128)(2,1)}) %all-reduce.2.cloned.1.call-update) | async-done | bytes 1572880 | tf_op jit(solution)/shard_map/psum | solution.py:42
  210.0 49.5 %all_to_all.19 = bf16[16,128,384]{2,1,0:T(8,128)(2,1)S(1)} all-to-all(bf16[16,128,384]{2,1,0:T(8,128)(2,1)} %all-reduce.2.cloned.1.call-done), channel_id=1, replica_groups=mesh['dp'=16,'tensor'=16] {'dp'}, dimensions={0} | all-to-all | bytes 3145728 | tf_op jit(solution)/shard_map/all_to_all | solution.py:43
  259.5 1.4 copy.13
  260.9 88.1 %reduce-scatter.4.cloned.1.call-done = bf16[384,1536]{1,0:T(8,128)(2,1)} async-done(((bf16[6144,1536]{1,0:T(8,128)(2,1)}), bf16[384,1536]{1,0:T(8,128)(2,1)}) %reduce-scatter.4.cloned.1.call-update) | async-done | bytes 1179664
  349.0 0.0 copy-start.1
  349.0 1.8 copy.12
  350.8 1.8 copy.10
  352.6 0.0 copy-done.1
Async XLA Ops:
  7.2 2.7 copy-start
  7.2 100.8 %all-gather.2.cloned.1.call-start = ((), (), s32[]{:S(2)}) async-start(), calls=%async_computation.2 | async-start | bytes 6684672 | tf_op jit(solution)/shard_map/all_gather | solution.py:37
  9.8 98.2 %copy-start.2 = (bf16[384,1536]{1,0:T(8,128)(2,1)S(1)}, bf16[384,1536]{1,0:T(8,128)(2,1)}, u32[]{:S(2)}) copy-start(bf16[384,1536]{1,0:T(8,128)(2,1)} %param.7) | copy-start | bytes 3538948
  9.8 200.2 %all-reduce.2.cloned.1.call-start = ((), (), s32[]{:S(2)}) async-start(), calls=%async_computation.3 | async-start | bytes 3145728 | tf_op jit(solution)/shard_map/psum | solution.py:42
  115.4 233.6 %reduce-scatter.4.cloned.1.call-start = ((), (), s32[]{:S(2)}) async-start(), calls=%async_computation.4 | async-start | bytes 20054016
  349.0 3.6 %copy-start.1 = (bf16[128,6144]{1,0:T(8,128)(2,1)S(1)}, bf16[128,6144]{1,0:T(8,128)(2,1)}, u32[]{:S(2)}) copy-start(bf16[128,6144]{1,0:T(8,128)(2,1)} %param.4) | copy-start | bytes 4718596
Sparse Core Ops, SparseCore 0:
  10.4 48.2 all-gather.1
  115.5 94.3 all-reduce.1
  212.5 136.4 reduce-scatter.3
where the time goes:
time: 363 us; the launch traced here: 359 us
  waiting for transfers between devices  137 us (38%)
  blocking collectives  130 us (36%)
  local copies, waits for them, and re-layouts  29.7 us (8%)
  matrix products  24.2 us (7%)
  other arithmetic  24 us (7%)
  between operations  14.5 us (4%)
    unnamed x4, waiting for transfers between devices  88.1 us
    pmax x1, blocking collectives, shared_max(): return lax.pmax(local_max, ('dp', 'tensor'))  80.6 us
    all_to_all x1, blocking collectives, on_device(): lax.all_to_all(summed, 'dp', split_axis=0, concat_axis=1, tiled=True)  49.5 us
    psum x1, waiting for transfers between devices, on_device(): summed = lax.psum(block_part.astype(jnp.bfloat16), 'tensor')  48.3 us
    unnamed x9, local copies, waits for them, and re-layouts  28.3 us
    convert_element_type x1, other arithmetic, on_device(): (partial_grad * grad_scale).astype(jnp.bfloat16)  21.5 us
    dot_general x1, matrix products, outer_rows(): lax.dot_general(left, right, (((0,), (0,)), ((), ())), preferred_element_...  16.8 us
    dot_general x1, matrix products, on_device(): lax.dot_general(all_pre, weight, (((1,), (1,)), ((), ())), preferred_elem...  7.39 us
  transfers between devices with their start and end apart: 3, of which 2 were waited for; matrix products, arithmetic and copies ran while one was open for 18% of the time, Pallas kernels for 0%

commit v1 on v0

v1 whole, which is shorter than its diff:
```python
import functools
import math

import jax
import jax.numpy as jnp
from jax import lax
from jax.experimental import pallas as pl
from jax.experimental.pallas import tpu as pltpu
from jax.sharding import PartitionSpec as P

gelu_coeff = math.sqrt(2.0 / math.pi)
epsilon = 1e-06

D, FF_DEV, TOK_DEV = 6144, 1536, 128
NZ, NT = 8, 16
HALF = TOK_DEV // 2
OWN = D // 16
CHIP = 2 * OWN
WIDE = CHIP + 128

VMEM = pl.BlockSpec(memory_space=pltpu.VMEM)
SMEM = pl.BlockSpec(memory_space=pltpu.SMEM)


def params(mib=48):
    return pltpu.CompilerParams(vmem_limit_bytes=mib << 20)


def dot(left, right, left_dim, right_dim):
    return lax.dot_general(
        left, right, (((left_dim,), (right_dim,)), ((), ())), preferred_element_type=jnp.float32
    )


def dev(z, c, t):
    return ((z % NZ) * 2 + c) * NT + t


def ring_perm(step):
    return [(z * 2 + c, ((z + step * (1 - 2 * c)) % NZ) * 2 + c) for z in range(NZ) for c in range(2)]


CORE_SWAP = [(d, d ^ 1) for d in range(2 * NZ)]


def spread_perm(sign):
    return [
        (dev(z, c, t), dev(z + sign * (1 - 2 * c) * (t >> 1), c, t))
        for z in range(NZ)
        for c in range(2)
        for t in range(NT)
    ]


def slope_kernel(pre_ref, act_ref, first_ref, second_ref):
    values = pre_ref[...].astype(jnp.float32)
    inner_arg = gelu_coeff * (values + 0.044715 * values * values * values)
    tanh_val = jnp.tanh(inner_arg)
    slope = 0.5 * (1.0 + tanh_val) + 0.5 * values * (1.0 - tanh_val * tanh_val) * gelu_coeff * (
        1.0 + 3.0 * 0.044715 * values * values
    )
    grad = (act_ref[...].astype(jnp.float32) * slope).astype(jnp.bfloat16)
    first_ref[...] = grad[:HALF]
    second_ref[...] = grad[HALF:]


def amax_kernel(in_ref, first_ref, second_ref, out_ref, grad, best):
    step = pl.program_id(0)

    @pl.when(step == 0)
    def _():
        grad[:HALF] = first_ref[...]
        grad[HALF:] = second_ref[...]
        best[...] = jnp.zeros_like(best)

    product = jnp.abs(dot(grad[...], in_ref[...], 0, 0))
    rows, cols = product.shape
    best[...] = jnp.maximum(best[...], jnp.max(product.reshape(rows // 8, 8, cols), axis=0))

    @pl.when(step == pl.num_programs(0) - 1)
    def _():
        out_ref[...] = jnp.full(out_ref.shape, jnp.max(best[...]), jnp.float32)


def block_kernel(*refs):
    chunks, (own_w, other_w, amax_ref, amax_other, out_ref, rows) = refs[:NT], refs[NT:]
    for n in range(NT):
        rows[n * HALF : (n + 1) * HALF] = chunks[n][...]
    for j, w in enumerate((own_w, other_w)):
        for part in range(2):
            span = pl.ds(part * 512, 512)
            product = dot(rows[span, :], w[...], 1, 1).astype(jnp.bfloat16)
            out_ref[part * 8 : part * 8 + 8, :, j * OWN : (j + 1) * OWN] = product.reshape(8, HALF, OWN)
    most = jnp.maximum(amax_ref[...], amax_other[...])[:1]
    high = most.astype(jnp.bfloat16)
    rest = most - high.astype(jnp.float32)
    mid = rest.astype(jnp.bfloat16)
    low = (rest - mid.astype(jnp.float32)).astype(jnp.bfloat16)
    for n in range(NT):
        for at, piece in enumerate((high, mid, low, low)):
            out_ref[n, at * 16 : at * 16 + 16, CHIP:] = jnp.broadcast_to(piece, (16, 128))


def joined(pieces):
    parts = [pieces[..., at * 16 : at * 16 + 1, :].astype(jnp.float32) for at in range(3)]
    return (parts[0] + parts[1]) + parts[2]


def sum_kernel(in_ref, out_ref):
    total = in_ref[0, :, :CHIP].astype(jnp.float32)
    for n in range(1, NT):
        total = total + in_ref[n, :, :CHIP].astype(jnp.float32)
    out_ref[:, :CHIP] = total.astype(jnp.bfloat16)
    most = joined(in_ref[0, :, CHIP:])
    for n in range(1, NT):
        most = jnp.maximum(most, joined(in_ref[n, :, CHIP:]))
    high = most.astype(jnp.bfloat16)
    rest = most - high.astype(jnp.float32)
    mid = rest.astype(jnp.bfloat16)
    low = (rest - mid.astype(jnp.float32)).astype(jnp.bfloat16)
    for at, piece in enumerate((high, mid, low, low)):
        out_ref[at * 16 : at * 16 + 16, CHIP:] = jnp.broadcast_to(piece, (16, 128))


def outer_kernel(*refs):
    chunks, (in_ref, own_ref, other_ref, rows) = refs[:NT], refs[NT:]
    for n in range(NT):
        rows[n * HALF : (n + 1) * HALF] = chunks[n][...]
    left = in_ref[...].reshape(NT * HALF, CHIP)
    own_ref[...] = dot(left[:, :OWN], rows[...], 0, 0)
    other_ref[...] = dot(left[:, OWN:], rows[...], 0, 0).astype(jnp.bfloat16)


def place_kernel(at_ref, in_ref, out_ref, amax_ref):
    z, c = at_ref[0], at_ref[1]
    for k in range(NZ):
        chip = lax.rem(z + (1 - 2 * c) * k + NZ, NZ)
        for j in range(2):
            side = c if j == 0 else 1 - c
            start = pl.multiple_of((chip * 2 + side) * OWN, 128)
            for h in range(2):
                out_ref[h * HALF : (h + 1) * HALF, pl.ds(start, OWN)] = in_ref[2 * k + h, :, j * OWN : (j + 1) * OWN]
    most = joined(in_ref[0, :, CHIP:])
    for n in range(1, NT):
        most = jnp.maximum(most, joined(in_ref[n, :, CHIP:]))
    amax_ref[...] = jnp.broadcast_to(most, amax_ref.shape)


def scale_kernel(own_ref, come_ref, amax_ref, out_ref):
    scale = 1.0 / (amax_ref[:1, :1] + epsilon)
    out_ref[...] = (own_ref[...] + come_ref[...].astype(jnp.float32)) * scale


def shape(dims, kind=jnp.bfloat16):
    return jax.ShapeDtypeStruct(dims, kind)


def on_device(inputs, preact, grad_act, weight):
    d, t = lax.axis_index("dp"), lax.axis_index("tensor")
    z, c = d // 2, d % 2
    k, half = t // 2, t % 2
    chip = (z + (1 - 2 * c) * k) % NZ
    pieces = [
        lax.dynamic_slice(inputs, (half * HALF, (chip * 2 + side) * OWN), (HALF, OWN)) for side in (c, 1 - c)
    ]
    sent = lax.ppermute(jnp.concatenate(pieces, axis=1), ("dp", "tensor"), spread_perm(1))
    in_all = lax.all_gather(sent, "tensor", axis=0)

    first, second = pl.pallas_call(
        slope_kernel,
        in_specs=[VMEM] * 2,
        out_specs=[VMEM] * 2,
        out_shape=[shape((HALF, FF_DEV))] * 2,
        compiler_params=params(),
        name="slope",
    )(preact, grad_act)
    other_w = lax.ppermute(weight, "dp", CORE_SWAP)

    chunks = {(0, 0): first, (0, 1): second}
    for step in range(1, 5):
        for sign, h in ((1, 0), (-1, 0), (1, 1), (-1, 1)):
            if step == 4 and (sign, h) in ((-1, 0), (1, 1)):
                continue
            before = chunks[((sign * (step - 1)) % NZ, h)]
            chunks[((sign * step) % NZ, h)] = lax.ppermute(before, "dp", ring_perm(sign))
    rows = [chunks[(n // 2, n % 2)] for n in range(NT)]

    amax = pl.pallas_call(
        amax_kernel,
        grid=(12,),
        in_specs=[
            pl.BlockSpec((TOK_DEV, 512), lambda n: (0, n)),
            pl.BlockSpec((HALF, FF_DEV), lambda n: (0, 0)),
            pl.BlockSpec((HALF, FF_DEV), lambda n: (0, 0)),
        ],
        out_specs=pl.BlockSpec((8, 128), lambda n: (0, 0)),
        out_shape=shape((8, 128), jnp.float32),
        scratch_shapes=[pltpu.VMEM((TOK_DEV, FF_DEV), jnp.bfloat16), pltpu.VMEM((8, 512), jnp.float32)],
        compiler_params=params(),
        cost_estimate=pl.CostEstimate(flops=2 * TOK_DEV * FF_DEV * D, bytes_accessed=2 << 20, transcendentals=0),
        name="amax",
    )(inputs, first, second)
    amax_other = lax.ppermute(amax, "dp", CORE_SWAP)

    block = pl.pallas_call(
        block_kernel,
        in_specs=[VMEM] * (NT + 4),
        out_specs=VMEM,
        out_shape=shape((NT, HALF, WIDE)),
        scratch_shapes=[pltpu.VMEM((NT * HALF, FF_DEV), jnp.bfloat16)],
        compiler_params=params(),
        cost_estimate=pl.CostEstimate(flops=2 * 1024 * FF_DEV * CHIP, bytes_accessed=7 << 20, transcendentals=0),
        name="block",
    )(*rows, weight, other_w, amax, amax_other)
    swapped = lax.all_to_all(block, "tensor", 0, 0)
    summed = pl.pallas_call(
        sum_kernel,
        in_specs=[VMEM],
        out_specs=VMEM,
        out_shape=shape((HALF, WIDE)),
        compiler_params=params(),
        name="sum",
    )(swapped)
    back = lax.ppermute(summed, ("dp", "tensor"), spread_perm(-1))

    own, other = pl.pallas_call(
        outer_kernel,
        in_specs=[VMEM] * (NT + 1),
        out_specs=[VMEM] * 2,
        out_shape=[shape((OWN, FF_DEV), jnp.float32), shape((OWN, FF_DEV))],
        scratch_shapes=[pltpu.VMEM((NT * HALF, FF_DEV), jnp.bfloat16)],
        compiler_params=params(),
        cost_estimate=pl.CostEstimate(flops=2 * 1024 * FF_DEV * CHIP, bytes_accessed=9 << 20, transcendentals=0),
        name="outer",
    )(*rows, in_all)
    come = lax.ppermute(other, "dp", CORE_SWAP)

    whole = lax.all_to_all(jnp.broadcast_to(back[None], (NT, HALF, WIDE)), "tensor", 0, 0)
    grad_input, grad_amax = pl.pallas_call(
        place_kernel,
        in_specs=[SMEM, VMEM],
        out_specs=[VMEM] * 2,
        out_shape=[shape((TOK_DEV, D)), shape((8, 128), jnp.float32)],
        compiler_params=params(),
        name="place",
    )(jnp.stack([z, c]).astype(jnp.int32), whole)
    weight_grad = pl.pallas_call(
        scale_kernel,
        in_specs=[VMEM] * 3,
        out_specs=VMEM,
        out_shape=shape((OWN, FF_DEV), jnp.float32),
        compiler_params=params(),
        name="scale",
    )(own, come, grad_amax)
    return (grad_input, weight_grad, grad_amax[0, 0])


def solution(mesh):
    placed = (P("dp", None), P("dp", "tensor"), P("dp", "tensor"), P("dp", "tensor"))
    return jax.shard_map(
        on_device,
        mesh=mesh,
        in_specs=placed,
        out_specs=(P("dp", None), P("dp", "tensor"), P()),
        check_vma=False,
    )
```

time: 363 us -> 161 us (0.44)
  waiting for transfers between devices: 137 us -> 25.9 us
  blocking collectives: 130 us -> 37.3 us
  starting transfers between devices: 0.12 us -> 38.6 us
  matrix products: 24.2 us -> 0 us
  other arithmetic: 24 us -> 0.09 us
  Pallas kernels: 0 us -> 23 us
  local copies, waits for them, and re-layouts: 29.7 us -> 21 us
    unnamed x4 -> x1, waiting for transfers between devices: 88.1 us -> 0.02 us
    pmax x1 -> x0, blocking collectives: 80.6 us -> none  [shared_max(): return lax.pmax(local_max, ('dp', 'tensor'))]
    psum x1 -> x0, waiting for transfers between devices: 48.3 us -> none  [on_device(): summed = lax.psum(block_part.astype(jnp.bfloat16), 'tensor')]
    dot_general x2 -> x0, matrix products: 24.2 us -> none  [the longest x1 16.8 us: outer_rows(): lax.dot_general(left, right, (((0,), (0,)), ((), ())), preferred_element_...]
    convert_element_type x2 -> x0, other arithmetic: 24 us -> none  [the longest x1 21.5 us: on_device(): (partial_grad * grad_scale).astype(jnp.bfloat16)]
    ppermute x0 -> x19, starting transfers between devices: none -> 23.9 us  [the longest x14 22.3 us: on_device(): chunks[sign * step % NZ, h] = lax.ppermute(before, 'dp', ring_perm(sign))]
    pallas_call x0 -> x7, Pallas kernels: none -> 23 us  [the longest x1 7.55 us: on_device(): pl.pallas_call(amax_kernel, grid=(12,), in_specs=[pl.BlockSpec((TOK_DEV,...]
    all_to_all x0 -> x1, starting transfers between devices: none -> 14.7 us  [on_device(): lax.all_to_all(jnp.broadcast_to(back[None], (NT, HALF, WIDE)), 'tensor',...]
  transfers between devices with their start and end apart: 3 -> 21, of which waited for: 2 -> 13; matrix products, arithmetic and copies ran while one was open for 18% -> 2% of each run, Pallas kernels for 0% -> 13%
where the time goes in v1:
time: 161 us; the launch traced here: 160 us
  starting transfers between devices  38.6 us (24%)
  blocking collectives  37.3 us (23%)
  waiting for transfers between devices  25.9 us (16%)
  Pallas kernels  23 us (14%)
  local copies, waits for them, and re-layouts  21 us (13%)
  between operations  14.2 us (9%)
    all_to_all x1, blocking collectives, on_device(): swapped = lax.all_to_all(block, 'tensor', 0, 0)  37.3 us
    ppermute x14, starting transfers between devices, on_device(): chunks[sign * step % NZ, h] = lax.ppermute(before, 'dp', ring_perm(sign))  22.3 us
    unnamed x46, local copies, waits for them, and re-layouts  18.1 us
    all_to_all x1, starting transfers between devices, on_device(): lax.all_to_all(jnp.broadcast_to(back[None], (NT, HALF, WIDE)), 'tensor',...  14.7 us
    ppermute x14, waiting for transfers between devices, on_device(): chunks[sign * step % NZ, h] = lax.ppermute(before, 'dp', ring_perm(sign))  12.4 us
    all_to_all x1, waiting for transfers between devices, on_device(): lax.all_to_all(jnp.broadcast_to(back[None], (NT, HALF, WIDE)), 'tensor',...  12.3 us
    pallas_call x1, Pallas kernels, on_device(): pl.pallas_call(amax_kernel, grid=(12,), in_specs=[pl.BlockSpec((TOK_DEV,...  7.55 us
    pallas_call x1, Pallas kernels, on_device(): pl.pallas_call(block_kernel, in_specs=[VMEM] * (NT + 4), out_specs=VMEM,...  5.68 us
  transfers between devices with their start and end apart: 21, of which 13 were waited for; matrix products, arithmetic and copies ran while one was open for 2% of the time, Pallas kernels for 13%

profile of v1, /device:TPU:32, one launch (start us, length us, event | category | flops | bytes accessed | tf_op | source)
XLA Modules:
  0.0 160.2 jit_solution(18206108843207778002)
XLA Ops:
  7.2 0.0 all-gather.3.cloned.1.call-start
  7.2 0.1 collective-permute-start.14
  7.4 0.8 fusion
  8.2 0.7 collective-permute-start.17
  8.9 0.0 copy-start.1
  8.9 1.0 copy-done.1
  9.9 1.0 copy-done.2
  10.9 0.6 slope.1
  11.5 1.9 %collective-permute-start.7 = (bf16[64,1536]{1,0:T(8,128)(2,1)S(1)}, bf16[64,1536]{1,0:T(8,128)(2,1)S(1)}, u32[]{:S(2)}, u32[]{:S(2)}) collective-permute-start(bf16[64,1536]{1,0:T(8,128)(2,1)S(1)} %get-tuple-element.10.second_ref.refs_1_), channel_id=1, source_target_pairs={{0,224},{16,48},{32,0},{48,80},{64,32},{80,112},{96,64},{112,144},... | collective-permute-start | bytes 589832 | tf_op jit(solution)/shard_map/ppermute | solution.py:185
  13.4 0.2 collective-permute-start
  13.6 1.4 copy-done.3
  15.0 7.5 %amax.1.refs_18_ = f32[8,128]{1,0:T(8,128)S(1)} custom-call(bf16[128,6144]{1,0:T(8,128)(2,1)S(1)} %copy-done.3, bf16[64,1536]{1,0:T(8,128)(2,1)S(1)} %get-tuple-element.9.first_ref.refs_0_, bf16[64,1536]{1,0:T(8,128)(2,1)S(1)} %get-tuple-element.10.second_ref.refs_1_), custom_call_target="tpu_custom_call" | custom-call | flops 2415919104 | bytes 2097152 | tf_op jit(solution)/shard_map/amax/pallas_call | solution.py:188
  22.5 0.1 collective-permute-start.15
  22.7 1.1 collective-permute-done.15.refs_19_
  23.8 3.9 %collective-permute-start.11 = (bf16[64,1536]{1,0:T(8,128)(2,1)S(1)}, bf16[64,1536]{1,0:T(8,128)(2,1)S(1)}, u32[]{:S(2)}, u32[]{:S(2)}) collective-permute-start(bf16[64,1536]{1,0:T(8,128)(2,1)S(1)} %get-tuple-element.9.first_ref.refs_0_), channel_id=1, source_target_pairs={{0,224},{16,48},{32,0},{48,80},{64,32},{80,112},{96,64},{112,144},... | collective-permute-start | bytes 589832 | tf_op jit(solution)/shard_map/ppermute | solution.py:185
  27.7 0.0 collective-permute-done.17
  27.7 0.6 copy-done.22
  28.4 0.0 collective-permute-start.1
  28.4 3.2 %collective-permute-start.8 = (bf16[64,1536]{1,0:T(8,128)(2,1)S(1)}, bf16[64,1536]{1,0:T(8,128)(2,1)}, u32[]{:S(2)}, u32[]{:S(2)}) collective-permute-start(bf16[64,1536]{1,0:T(8,128)(2,1)S(1)} %collective-permute-done.7.refs_15_), channel_id=1, source_target_pairs={{0,224},{16,48},{32,0},{48,80},{64,32},{80,112},{96,64},{112,144},... | collective-permute-start | bytes 589832 | tf_op jit(solution)/shard_map/ppermute | solution.py:185
  31.6 0.0 all-gather.3.cloned.1.call-update
  31.7 1.4 collective-permute-done.11.refs_14_
  33.0 3.2 %collective-permute-start.12 = (bf16[64,1536]{1,0:T(8,128)(2,1)S(1)}, bf16[64,1536]{1,0:T(8,128)(2,1)S(1)}, u32[]{:S(2)}, u32[]{:S(2)}) collective-permute-start(bf16[64,1536]{1,0:T(8,128)(2,1)S(1)} %collective-permute-done.11.refs_14_), channel_id=1, source_target_pairs={{0,224},{16,48},{32,0},{48,80},{64,32},{80,112},{96,64},{112,144},... | collective-permute-start | bytes 589832 | tf_op jit(solution)/shard_map/ppermute | solution.py:185
  36.3 1.1 collective-permute-done.1.refs_3_
  37.3 3.3 %collective-permute-start.9 = (bf16[64,1536]{1,0:T(8,128)(2,1)}, bf16[64,1536]{1,0:T(8,128)(2,1)S(1)}, u32[]{:S(2)}, u32[]{:S(2)}) collective-permute-start(bf16[64,1536]{1,0:T(8,128)(2,1)} %collective-permute-done.8.refs_13_), channel_id=1, source_target_pairs={{0,224},{16,48},{32,0},{48,80},{64,32},{80,112},{96,64},{112,144},... | collective-permute-start | bytes 589832 | tf_op jit(solution)/shard_map/ppermute | solution.py:185
  40.6 0.4 collective-permute-done.2.refs_4_
  41.1 0.6 collective-permute-done.12.refs_12_
  41.6 2.9 %collective-permute-start.13 = (bf16[64,1536]{1,0:T(8,128)(2,1)S(1)}, bf16[64,1536]{1,0:T(8,128)(2,1)S(1)}, u32[]{:S(2)}, u32[]{:S(2)}) collective-permute-start(bf16[64,1536]{1,0:T(8,128)(2,1)S(1)} %collective-permute-done.12.refs_12_), channel_id=1, source_target_pairs={{0,224},{16,48},{32,0},{48,80},{64,32},{80,112},{96,64},{112,144},... | collective-permute-start | bytes 589832 | tf_op jit(solution)/shard_map/ppermute | solution.py:185
  44.5 0.7 collective-permute-done.3.refs_5_
  45.3 1.0 collective-permute-done.9.refs_11_
  46.3 3.6 %collective-permute-start.10 = (bf16[64,1536]{1,0:T(8,128)(2,1)S(1)}, bf16[64,1536]{1,0:T(8,128)(2,1)S(1)}, u32[]{:S(2)}, u32[]{:S(2)}) collective-permute-start(bf16[64,1536]{1,0:T(8,128)(2,1)S(1)} %collective-permute-done.9.refs_11_), channel_id=1, source_target_pairs={{0,224},{16,48},{32,0},{48,80},{64,32},{80,112},{96,64},{112,144},... | collective-permute-start | bytes 589832 | tf_op jit(solution)/shard_map/ppermute | solution.py:185
  49.9 0.3 collective-permute-done.4.refs_6_
  50.2 0.2 collective-permute-done.13.refs_10_
  50.4 3.0 %collective-permute-done.5.refs_7_ = bf16[64,1536]{1,0:T(8,128)(2,1)S(1)} collective-permute-done((bf16[64,1536]{1,0:T(8,128)(2,1)S(1)}, bf16[64,1536]{1,0:T(8,128)(2,1)S(1)}, u32[]{:S(2)}, u32[]{:S(2)}) %collective-permute-start.5) | collective-permute-done | bytes 196640 | tf_op jit(solution)/shard_map/ppermute | solution.py:185
  53.4 0.6 collective-permute-done.10.refs_9_
  54.0 3.1 %collective-permute-done.6.refs_8_ = bf16[64,1536]{1,0:T(8,128)(2,1)S(1)} collective-permute-done((bf16[64,1536]{1,0:T(8,128)(2,1)S(1)}, bf16[64,1536]{1,0:T(8,128)(2,1)S(1)}, u32[]{:S(2)}, u32[]{:S(2)}) %collective-permute-start.6) | collective-permute-done | bytes 196640 | tf_op jit(solution)/shard_map/ppermute | solution.py:185
  57.2 5.7 %block.1 = bf16[16,64,896]{2,1,0:T(8,128)(2,1)} custom-call(bf16[64,1536]{1,0:T(8,128)(2,1)S(1)} %get-tuple-element.9.first_ref.refs_0_, bf16[64,1536]{1,0:T(8,128)(2,1)S(1)} %get-tuple-element.10.second_ref.refs_1_, bf16[64,1536]{1,0:T(8,128)(2,1)S(1)} %collective-permute-done.refs_2_, bf16[64,1536]{1,0:T(8,128)(2,1)S(1)} %collective-permute-done.1.refs_3_, ...), custom_call_target="tpu_custom_call" | custom-call | flops 2415919104 | bytes 7340032 | tf_op jit(solution)/shard_map/block/pallas_call | solution.py:205
  62.8 0.7 copy-done.6
  63.5 0.7 copy-done.8
  64.2 0.7 copy-done.10
  64.9 0.7 copy-done.12
  65.6 0.7 copy-done.14
  66.3 0.7 copy-done.16
  66.9 0.7 copy-done.18
  67.6 0.7 copy-done.20
  68.3 37.3 %all_to_all.10.in_ref = bf16[16,64,896]{2,1,0:T(8,128)(2,1)S(1)} all-to-all(bf16[16,64,896]{2,1,0:T(8,128)(2,1)} %block.1), channel_id=1, replica_groups=mesh['dp'=16,'tensor'=16] {'tensor'}, dimensions={0} | all-to-all | bytes 3670016 | tf_op jit(solution)/shard_map/all_to_all | solution.py:215
  105.6 0.2 sum.1
  105.8 0.7 collective-permute-start.16
  106.5 1.5 broadcast_in_dim.2
  108.0 14.7 %all-to-all-start.1 = ((bf16[16,64,896]{2,1,0:T(8,128)(2,1)}), bf16[16,64,896]{2,1,0:T(8,128)(2,1)S(1)}, u32[]{:S(2)}, u32[]{:S(2)}) async-start(bf16[16,64,896]{2,1,0:T(8,128)(2,1)} %broadcast_in_dim.2), calls=%async_computation.1 | async-start | bytes 3670016 | tf_op jit(solution)/shard_map/all_to_all | solution.py:238
  122.7 0.0 all-gather.3.cloned.1.call-done
  122.8 1.4 copy-done.4
  124.2 0.9 copy-done.11
  125.1 0.9 copy-done.13
  126.0 0.9 copy-done.15
  127.0 0.9 copy-done.17
  127.9 0.9 copy-done.19
  128.8 0.9 copy-done.21
  129.8 5.2 %outer.1 = (f32[384,1536]{1,0:T(8,128)}, bf16[384,1536]{1,0:T(8,128)(2,1)}) custom-call(bf16[64,1536]{1,0:T(8,128)(2,1)S(1)} %get-tuple-element.9.first_ref.refs_0_, bf16[64,1536]{1,0:T(8,128)(2,1)S(1)} %get-tuple-element.10.second_ref.refs_1_, bf16[64,1536]{1,0:T(8,128)(2,1)S(1)} %collective-permute-done.refs_2_, ...), custom_call_target="tpu_custom_call" | custom-call | flops 2415919104 | bytes 9437184 | tf_op jit(solution)/shard_map/outer/pallas_call | solution.py:226
  134.9 0.1 pad_add_fusion.at_ref
  135.0 12.3 %all-to-all-done.1.in_ref = bf16[16,64,896]{2,1,0:T(8,128)(2,1)S(1)} async-done(((bf16[16,64,896]{2,1,0:T(8,128)(2,1)}), bf16[16,64,896]{2,1,0:T(8,128)(2,1)S(1)}, u32[]{:S(2)}, u32[]{:S(2)}) %all-to-all-start.1) | async-done | bytes 1835040 | tf_op jit(solution)/shard_map/all_to_all | solution.py:238
  147.3 1.8 %place.1 = (bf16[128,6144]{1,0:T(8,128)(2,1)}, f32[8,128]{1,0:T(8,128)S(1)}) custom-call(s32[2]{0:T(128)S(1)} %pad_add_fusion.at_ref, bf16[16,64,896]{2,1,0:T(8,128)(2,1)S(1)} %all-to-all-done.1.in_ref), custom_call_target="tpu_custom_call" | custom-call | tf_op jit(solution)/shard_map/place/pallas_call | solution.py:239
  149.2 0.5 slice.3
  149.7 1.7 %copy-done = f32[384,1536]{1,0:T(8,128)S(1)} copy-done((f32[384,1536]{1,0:T(8,128)S(1)}, f32[384,1536]{1,0:T(8,128)}, u32[]{:S(2)}) %copy-start) | copy-done | bytes 2359320
  151.4 2.0 %scale.1 = f32[384,1536]{1,0:T(8,128)} custom-call(f32[384,1536]{1,0:T(8,128)S(1)} %copy-done, bf16[384,1536]{1,0:T(8,128)(2,1)S(1)} %collective-permute-done.18.come_ref, f32[8,128]{1,0:T(8,128)S(1)} %get-tuple-element.14.amax_ref), custom_call_target="tpu_custom_call" | custom-call | tf_op jit(solution)/shard_map/scale/pallas_call | solution.py:247
  (38 shorter events, 0.1 us)
Async XLA Ops:
  7.2 115.6 %all-gather.3.cloned.1.call-start = ((), (), s32[]{:S(2)}) async-start(), calls=%async_computation.2 | async-start | bytes 1671168 | tf_op jit(solution)/shard_map/all_gather | solution.py:167
  7.2 49.9 %collective-permute-start.14 = (bf16[384,1536]{1,0:T(8,128)(2,1)}, bf16[384,1536]{1,0:T(8,128)(2,1)S(1)}, u32[]{:S(2)}, u32[]{:S(2)}) collective-permute-start(bf16[384,1536]{1,0:T(8,128)(2,1)} %refs_16_.1), channel_id=1, source_target_pairs={{0,16},{16,0},{32,48},{48,32},{64,80},{80,64},{96,112},{112,96},{1... | collective-permute-start | bytes 3538952 | tf_op jit(solution)/shard_map/ppermute | solution.py:177
  8.2 19.5 %collective-permute-start.17 = (bf16[64,768]{1,0:T(8,128)(2,1)S(1)}, bf16[64,768]{1,0:T(8,128)(2,1)S(1)}, u32[]{:S(2)}, u32[]{:S(2)}) collective-permute-start(bf16[64,768]{1,0:T(8,128)(2,1)S(1)} %pad_maximum_fusion), channel_id=1, source_target_pairs={{0,0},{1,1},{2,34},{3,35},{4,68},{5,69},{6,102},{7,103},{8,136},{9... | collective-permute-start | bytes 294920 | tf_op jit(solution)/shard_map/ppermute | solution.py:166
  8.9 1.0 copy-start.1
  9.9 1.0 copy-start.2
  11.5 16.9 %collective-permute-start.7 = (bf16[64,1536]{1,0:T(8,128)(2,1)S(1)}, bf16[64,1536]{1,0:T(8,128)(2,1)S(1)}, u32[]{:S(2)}, u32[]{:S(2)}) collective-permute-start(bf16[64,1536]{1,0:T(8,128)(2,1)S(1)} %get-tuple-element.10.second_ref.refs_1_), channel_id=1, source_target_pairs={{0,224},{16,48},{32,0},{48,80},{64,32},{80,112},{96,64},{112,144},... | collective-permute-start | bytes 589832 | tf_op jit(solution)/shard_map/ppermute | solution.py:185
  13.4 18.2 %collective-permute-start = (bf16[64,1536]{1,0:T(8,128)(2,1)S(1)}, bf16[64,1536]{1,0:T(8,128)(2,1)S(1)}, u32[]{:S(2)}, u32[]{:S(2)}) collective-permute-start(bf16[64,1536]{1,0:T(8,128)(2,1)S(1)} %get-tuple-element.9.first_ref.refs_0_), channel_id=1, source_target_pairs={{0,32},{16,240},{32,64},{48,16},{64,96},{80,48},{96,128},{112,80},... | collective-permute-start | bytes 589832 | tf_op jit(solution)/shard_map/ppermute | solution.py:185
  13.6 1.4 copy-start.3
  15.0 42.2 %copy-start.5 = (bf16[384,1536]{1,0:T(8,128)(2,1)S(1)}, bf16[384,1536]{1,0:T(8,128)(2,1)}, u32[]{:S(2)}) copy-start(bf16[384,1536]{1,0:T(8,128)(2,1)} %refs_16_.1) | copy-start | bytes 3538948
  22.5 1.3 collective-permute-start.15
  23.8 9.2 %collective-permute-start.11 = (bf16[64,1536]{1,0:T(8,128)(2,1)S(1)}, bf16[64,1536]{1,0:T(8,128)(2,1)S(1)}, u32[]{:S(2)}, u32[]{:S(2)}) collective-permute-start(bf16[64,1536]{1,0:T(8,128)(2,1)S(1)} %get-tuple-element.9.first_ref.refs_0_), channel_id=1, source_target_pairs={{0,224},{16,48},{32,0},{48,80},{64,32},{80,112},{96,64},{112,144},... | collective-permute-start | bytes 589832 | tf_op jit(solution)/shard_map/ppermute | solution.py:185
  27.7 0.6 copy-start.22
  28.4 9.0 %collective-permute-start.1 = (bf16[64,1536]{1,0:T(8,128)(2,1)S(1)}, bf16[64,1536]{1,0:T(8,128)(2,1)S(1)}, u32[]{:S(2)}, u32[]{:S(2)}) collective-permute-start(bf16[64,1536]{1,0:T(8,128)(2,1)S(1)} %get-tuple-element.10.second_ref.refs_1_), channel_id=1, source_target_pairs={{0,32},{16,240},{32,64},{48,16},{64,96},{80,48},{96,128},{112,80},... | collective-permute-start | bytes 589832 | tf_op jit(solution)/shard_map/ppermute | solution.py:185
  28.4 9.0 %collective-permute-start.8 = (bf16[64,1536]{1,0:T(8,128)(2,1)S(1)}, bf16[64,1536]{1,0:T(8,128)(2,1)}, u32[]{:S(2)}, u32[]{:S(2)}) collective-permute-start(bf16[64,1536]{1,0:T(8,128)(2,1)S(1)} %collective-permute-done.7.refs_15_), channel_id=1, source_target_pairs={{0,224},{16,48},{32,0},{48,80},{64,32},{80,112},{96,64},{112,144},... | collective-permute-start | bytes 589832 | tf_op jit(solution)/shard_map/ppermute | solution.py:185
  31.6 9.4 %collective-permute-start.2 = (bf16[64,1536]{1,0:T(8,128)(2,1)S(1)}, bf16[64,1536]{1,0:T(8,128)(2,1)}, u32[]{:S(2)}, u32[]{:S(2)}) collective-permute-start(bf16[64,1536]{1,0:T(8,128)(2,1)S(1)} %collective-permute-done.refs_2_), channel_id=1, source_target_pairs={{0,32},{16,240},{32,64},{48,16},{64,96},{80,48},{96,128},{112,80},... | collective-permute-start | bytes 589832 | tf_op jit(solution)/shard_map/ppermute | solution.py:185
  33.0 8.6 %collective-permute-start.12 = (bf16[64,1536]{1,0:T(8,128)(2,1)S(1)}, bf16[64,1536]{1,0:T(8,128)(2,1)S(1)}, u32[]{:S(2)}, u32[]{:S(2)}) collective-permute-start(bf16[64,1536]{1,0:T(8,128)(2,1)S(1)} %collective-permute-done.11.refs_14_), channel_id=1, source_target_pairs={{0,224},{16,48},{32,0},{48,80},{64,32},{80,112},{96,64},{112,144},... | collective-permute-start | bytes 589832 | tf_op jit(solution)/shard_map/ppermute | solution.py:185
  37.3 7.9 %collective-permute-start.3 = (bf16[64,1536]{1,0:T(8,128)(2,1)S(1)}, bf16[64,1536]{1,0:T(8,128)(2,1)S(1)}, u32[]{:S(2)}, u32[]{:S(2)}) collective-permute-start(bf16[64,1536]{1,0:T(8,128)(2,1)S(1)} %collective-permute-done.1.refs_3_), channel_id=1, source_target_pairs={{0,32},{16,240},{32,64},{48,16},{64,96},{80,48},{96,128},{112,80},... | collective-permute-start | bytes 589832 | tf_op jit(solution)/shard_map/ppermute | solution.py:185
  37.3 9.0 %collective-permute-start.9 = (bf16[64,1536]{1,0:T(8,128)(2,1)}, bf16[64,1536]{1,0:T(8,128)(2,1)S(1)}, u32[]{:S(2)}, u32[]{:S(2)}) collective-permute-start(bf16[64,1536]{1,0:T(8,128)(2,1)} %collective-permute-done.8.refs_13_), channel_id=1, source_target_pairs={{0,224},{16,48},{32,0},{48,80},{64,32},{80,112},{96,64},{112,144},... | collective-permute-start | bytes 589832 | tf_op jit(solution)/shard_map/ppermute | solution.py:185
  41.1 9.2 %collective-permute-start.4 = (bf16[64,1536]{1,0:T(8,128)(2,1)}, bf16[64,1536]{1,0:T(8,128)(2,1)S(1)}, u32[]{:S(2)}, u32[]{:S(2)}) collective-permute-start(bf16[64,1536]{1,0:T(8,128)(2,1)} %collective-permute-done.2.refs_4_), channel_id=1, source_target_pairs={{0,32},{16,240},{32,64},{48,16},{64,96},{80,48},{96,128},{112,80},... | collective-permute-start | bytes 589832 | tf_op jit(solution)/shard_map/ppermute | solution.py:185
  41.6 8.8 %collective-permute-start.13 = (bf16[64,1536]{1,0:T(8,128)(2,1)S(1)}, bf16[64,1536]{1,0:T(8,128)(2,1)S(1)}, u32[]{:S(2)}, u32[]{:S(2)}) collective-permute-start(bf16[64,1536]{1,0:T(8,128)(2,1)S(1)} %collective-permute-done.12.refs_12_), channel_id=1, source_target_pairs={{0,224},{16,48},{32,0},{48,80},{64,32},{80,112},{96,64},{112,144},... | collective-permute-start | bytes 589832 | tf_op jit(solution)/shard_map/ppermute | solution.py:185
  45.3 8.1 %collective-permute-start.5 = (bf16[64,1536]{1,0:T(8,128)(2,1)S(1)}, bf16[64,1536]{1,0:T(8,128)(2,1)S(1)}, u32[]{:S(2)}, u32[]{:S(2)}) collective-permute-start(bf16[64,1536]{1,0:T(8,128)(2,1)S(1)} %collective-permute-done.3.refs_5_), channel_id=1, source_target_pairs={{0,32},{16,240},{32,64},{48,16},{64,96},{80,48},{96,128},{112,80},... | collective-permute-start | bytes 589832 | tf_op jit(solution)/shard_map/ppermute | solution.py:185
  46.3 7.7 %collective-permute-start.10 = (bf16[64,1536]{1,0:T(8,128)(2,1)S(1)}, bf16[64,1536]{1,0:T(8,128)(2,1)S(1)}, u32[]{:S(2)}, u32[]{:S(2)}) collective-permute-start(bf16[64,1536]{1,0:T(8,128)(2,1)S(1)} %collective-permute-done.9.refs_11_), channel_id=1, source_target_pairs={{0,224},{16,48},{32,0},{48,80},{64,32},{80,112},{96,64},{112,144},... | collective-permute-start | bytes 589832 | tf_op jit(solution)/shard_map/ppermute | solution.py:185
  50.2 6.9 %collective-permute-start.6 = (bf16[64,1536]{1,0:T(8,128)(2,1)S(1)}, bf16[64,1536]{1,0:T(8,128)(2,1)S(1)}, u32[]{:S(2)}, u32[]{:S(2)}) collective-permute-start(bf16[64,1536]{1,0:T(8,128)(2,1)S(1)} %collective-permute-done.4.refs_6_), channel_id=1, source_target_pairs={{0,32},{16,240},{32,64},{48,16},{64,96},{80,48},{96,128},{112,80},... | collective-permute-start | bytes 589832 | tf_op jit(solution)/shard_map/ppermute | solution.py:185
  62.8 0.7 copy-start.6
  63.5 0.7 copy-start.8
  64.2 0.7 copy-start.10
  64.9 0.7 copy-start.12
  65.6 0.7 copy-start.14
  66.3 0.7 copy-start.16
  66.9 0.7 copy-start.18
  67.6 0.7 copy-start.20
  105.8 0.7 collective-permute-start.16
  108.0 14.7 %copy-start.7 = (bf16[64,1536]{1,0:T(8,128)(2,1)S(1)}, bf16[64,1536]{1,0:T(8,128)(2,1)}, u32[]{:S(2)}) copy-start(bf16[64,1536]{1,0:T(8,128)(2,1)} %copy-done.6) | copy-start | bytes 589828
  108.0 14.7 %copy-start.9 = (bf16[64,1536]{1,0:T(8,128)(2,1)S(1)}, bf16[64,1536]{1,0:T(8,128)(2,1)}, u32[]{:S(2)}) copy-start(bf16[64,1536]{1,0:T(8,128)(2,1)} %copy-done.8) | copy-start | bytes 589828
  108.0 39.3 %all-to-all-start.1 = ((bf16[16,64,896]{2,1,0:T(8,128)(2,1)}), bf16[16,64,896]{2,1,0:T(8,128)(2,1)S(1)}, u32[]{:S(2)}, u32[]{:S(2)}) async-start(bf16[16,64,896]{2,1,0:T(8,128)(2,1)} %broadcast_in_dim.2), calls=%async_computation.1 | async-start | bytes 3670016 | tf_op jit(solution)/shard_map/all_to_all | solution.py:238
  122.8 1.4 copy-start.4
  124.2 0.9 copy-start.11
  125.1 0.9 copy-start.13
  126.0 0.9 copy-start.15
  127.0 0.9 copy-start.17
  127.9 0.9 copy-start.19
  128.8 0.9 copy-start.21
  134.9 14.8 %collective-permute-start.18 = (bf16[384,1536]{1,0:T(8,128)(2,1)}, bf16[384,1536]{1,0:T(8,128)(2,1)S(1)}, u32[]{:S(2)}, u32[]{:S(2)}) collective-permute-start(bf16[384,1536]{1,0:T(8,128)(2,1)} %get-tuple-element.13), channel_id=1, source_target_pairs={{0,16},{16,0},{32,48},{48,32},{64,80},{80,64},{96,112},{112,96},{1... | collective-permute-start | bytes 3538952 | tf_op jit(solution)/shard_map/ppermute | solution.py:236
  149.7 1.7 %copy-start = (f32[384,1536]{1,0:T(8,128)S(1)}, f32[384,1536]{1,0:T(8,128)}, u32[]{:S(2)}) copy-start(f32[384,1536]{1,0:T(8,128)} %get-tuple-element.12.own_ref) | copy-start | bytes 7077892
Sparse Core Ops, SparseCore 0:
  31.8 59.8 all-gather.2

commit v2 on v0

v2 whole, which is shorter than its diff:
```python
import functools
import math

import jax
import jax.numpy as jnp
from jax import lax
from jax.experimental import pallas as pl
from jax.experimental.pallas import tpu as pltpu
from jax.sharding import PartitionSpec as P

gelu_coeff = math.sqrt(2.0 / math.pi)
epsilon = 1e-06

D, FF_DEV, TOK_DEV = 6144, 1536, 128
NZ, NT = 8, 16
HALF = TOK_DEV // 2
OWN = D // 16
CHIP = 2 * OWN
LANES = 128
WIDE = CHIP + LANES

VMEM = pl.BlockSpec(memory_space=pltpu.VMEM)
HBM = pl.BlockSpec(memory_space=pltpu.HBM)
SMEM = pl.BlockSpec(memory_space=pltpu.SMEM)


def params(mib):
    return pltpu.CompilerParams(vmem_limit_bytes=mib << 20)


def dot(left, right, left_dim, right_dim):
    return lax.dot_general(
        left, right, (((left_dim,), (right_dim,)), ((), ())), preferred_element_type=jnp.float32
    )


def dev(z, c, t):
    return ((z % NZ) * 2 + c) * NT + t


def ring_perm(step):
    return [(z * 2 + c, ((z + step * (1 - 2 * c)) % NZ) * 2 + c) for z in range(NZ) for c in range(2)]


CORE_SWAP = [(d, d ^ 1) for d in range(2 * NZ)]


def shift_of(c, k):
    return k - 4 * c


def block_of(c, k):
    return lax.rem((1 - 2 * c) * k + 4 * c + NZ, NZ)


def spread_perm(sign):
    return [
        (dev(z, c, t), dev(z + sign * shift_of(c, t >> 1), c, t))
        for z in range(NZ)
        for c in range(2)
        for t in range(NT)
    ]


def fetch(pairs, sems):
    copies = [pltpu.make_async_copy(src, dst, sems.at[n]) for n, (src, dst) in enumerate(pairs)]
    for copy in copies:
        copy.start()
    return copies


def slope_kernel(pre_hbm, act_hbm, first_ref, second_ref, pre, act, sems):
    for copy in fetch([(pre_hbm, pre), (act_hbm, act)], sems):
        copy.wait()
    values = pre[...].astype(jnp.float32)
    inner_arg = gelu_coeff * (values + 0.044715 * values * values * values)
    tanh_val = jnp.tanh(inner_arg)
    slope = 0.5 * (1.0 + tanh_val) + 0.5 * values * (1.0 - tanh_val * tanh_val) * gelu_coeff * (
        1.0 + 3.0 * 0.044715 * values * values
    )
    grad = (act[...].astype(jnp.float32) * slope).astype(jnp.bfloat16)
    first_ref[...] = grad[:HALF]
    second_ref[...] = grad[HALF:]


def pieces_of(most):
    high = most.astype(jnp.bfloat16).astype(jnp.float32)
    mid = (most - high).astype(jnp.bfloat16).astype(jnp.float32)
    low = (most - high) - mid
    row = lax.broadcasted_iota(jnp.int32, (16, LANES), 0)
    return jnp.where(row == 0, high, jnp.where(row == 1, mid, low)).astype(jnp.bfloat16)


def joined(pieces):
    wide = pieces.astype(jnp.float32)
    return (wide[..., 0:1, :] + wide[..., 1:2, :]) + wide[..., 2:3, :]


def amax_kernel(part, before_ref, in_ref, first_ref, second_ref, out_ref):
    width = D // AMAX_PARTS
    best = jnp.zeros((8, 256), jnp.float32)
    for i in range(FF_DEV // 256):
        span = slice(i * 256, (i + 1) * 256)
        left = jnp.concatenate([first_ref[:, span], second_ref[:, span]], axis=0).T
        for j in range(width // 256):
            features = in_ref[:, part * width + j * 256 : part * width + (j + 1) * 256]
            product = jnp.abs(dot(left, features, 1, 0))
            best = jnp.maximum(best, jnp.max(product.reshape(32, 8, 256), axis=0))
    out_ref[...] = jnp.maximum(before_ref[...], jnp.max(best))


def pick_kernel(at_ref, in_hbm, *refs):
    outs, (tokens, made, sems) = refs[:NZ], refs[NZ:]
    z, c, h = at_ref[0], at_ref[1], at_ref[2]
    load = pltpu.make_async_copy(in_hbm.at[pl.ds(pl.multiple_of(h * HALF, HALF), HALF)], tokens, sems.at[NZ])
    load.start()
    load.wait()
    sent = []
    for k in range(NZ):
        chip = lax.rem(z + (1 - 2 * c) * k + NZ, NZ)
        for j in range(2):
            side = c if j == 0 else 1 - c
            start = pl.multiple_of((chip * 2 + side) * OWN, LANES)
            made[k, :, j * OWN : (j + 1) * OWN] = tokens[:, pl.ds(start, OWN)]
        sent.append(pltpu.make_async_copy(made.at[k], outs[k], sems.at[k]))
        sent[-1].start()
    for copy in sent:
        copy.wait()


def stack_kernel(*refs):
    pieces, (out_ref, token_ref, sems) = refs[:NZ], refs[NZ:]
    copies = fetch([(piece, out_ref.at[k]) for k, piece in enumerate(pieces)], sems)
    token_ref[...] = jnp.zeros_like(token_ref)
    for copy in copies:
        copy.wait()


def tie_kernel(*refs):
    pass


def gate_kernel(*refs):
    refs[-1][...] = jnp.zeros_like(refs[-1])


def block_kernel(*refs):
    at_ref, chunks = refs[0], refs[1 : NT + 1]
    own_w, other_w, amax_ref, amax_other, out_hbm, rows, weights, made, sems, out_sems = refs[NT + 1 :]
    c = at_ref[1]
    copies = fetch(
        [(own_w, weights.at[0])]
        + [(chunk, rows.at[pl.ds(n * HALF, HALF)]) for n, chunk in enumerate(chunks)]
        + [(other_w, weights.at[1])],
        sems,
    )
    lanes = pieces_of(jnp.maximum(amax_ref[...], amax_other[...])[:1])
    for n in range(NT):
        for q in range(HALF // 16):
            made[n, q * 16 : q * 16 + 16, CHIP:] = lanes
    outs = []
    for j in range(2):
        copies[j * (NT + 1)].wait()
        for group in range(4):
            if j == 0:
                for n in range(4 * group, 4 * group + 4):
                    copies[1 + n].wait()
            left = rows[4 * group * HALF : 4 * (group + 1) * HALF]
            product = dot(left, weights[j], 1, 1).astype(jnp.bfloat16).reshape(4, HALF, OWN)
            made[4 * group : 4 * group + 4, :, j * OWN : (j + 1) * OWN] = product
            if j == 0:
                continue
            for k in (2 * group, 2 * group + 1):
                there = out_hbm.at[pl.ds(2 * block_of(c, k), 2)]
                outs.append(pltpu.make_async_copy(made.at[pl.ds(2 * k, 2)], there, out_sems.at[k]))
                outs[-1].start()
    for copy in outs:
        copy.wait()


def sum_kernel(in_ref, _, out_ref):
    total = in_ref[0, :, :CHIP].astype(jnp.float32)
    for n in range(1, NT):
        total = total + in_ref[n, :, :CHIP].astype(jnp.float32)
    out_ref[:, :CHIP] = total.astype(jnp.bfloat16)
    most = joined(in_ref[0, :16, CHIP:])
    for n in range(1, NT):
        most = jnp.maximum(most, joined(in_ref[n, :16, CHIP:]))
    for q in range(HALF // 16):
        out_ref[q * 16 : q * 16 + 16, CHIP:] = pieces_of(most)


def spread_kernel(in_ref, _, out_ref, token_ref):
    for n in range(NT):
        out_ref[n] = in_ref[...]
    token_ref[...] = jnp.zeros_like(token_ref)


def outer_kernel(at_ref, _, *refs):
    chunks = refs[:NT]
    mine_ref, theirs_ref, own_ref, other_ref, rows, left = refs[NT:]
    for n in range(NT):
        rows[n * HALF : (n + 1) * HALF] = chunks[n][...]
    for h, (one, two) in enumerate(((mine_ref, theirs_ref), (theirs_ref, mine_ref))):

        @pl.when(at_ref[2] == h)
        def _(one=one, two=two):
            for k in range(NZ):
                left[k * TOK_DEV : k * TOK_DEV + HALF] = one[k]
                left[k * TOK_DEV + HALF : (k + 1) * TOK_DEV] = two[k]

    other_ref[...] = dot(left[:, OWN:], rows[...], 0, 0).astype(jnp.bfloat16)
    own_ref[...] = dot(left[:, :OWN], rows[...], 0, 0).astype(jnp.bfloat16)


def final_kernel(
    at_ref, whole_hbm, own_hbm, come_hbm, gi_hbm, wg_hbm, amax_ref, whole, gi, own, come, made, sems
):
    whole_in, own_in, come_in = fetch([(whole_hbm, whole), (own_hbm, own), (come_hbm, come)], sems)
    z, c = at_ref[0], at_ref[1]
    whole_in.wait()
    most = joined(whole[0, :16, CHIP:])
    for n in range(1, NT):
        most = jnp.maximum(most, joined(whole[n, :16, CHIP:]))
    amax_ref[0, 0] = jnp.max(most)
    for k in range(NZ):
        chip = lax.rem(z + shift_of(c, k) + NZ, NZ)
        for j in range(2):
            side = c if j == 0 else 1 - c
            start = pl.multiple_of((chip * 2 + side) * OWN, LANES)
            for h in range(2):
                gi[h * HALF : (h + 1) * HALF, pl.ds(start, OWN)] = whole[2 * k + h, :, j * OWN : (j + 1) * OWN]
    outs = [pltpu.make_async_copy(gi, gi_hbm, sems.at[6])]
    outs[0].start()
    scale = 1.0 / (most[:, :1] + epsilon)
    own_in.wait()
    come_in.wait()
    for n in range(4):
        span = pl.ds(n * (OWN // 4), OWN // 4)
        made[span, :] = (own[span, :].astype(jnp.float32) + come[span, :].astype(jnp.float32)) * scale
        outs.append(pltpu.make_async_copy(made.at[span], wg_hbm.at[span], sems.at[2 + n]))
        outs[-1].start()
    for copy in outs:
        copy.wait()


def shape(dims, kind=jnp.bfloat16):
    return jax.ShapeDtypeStruct(dims, kind)


def cost(flops, moved):
    return pl.CostEstimate(flops=flops, bytes_accessed=moved, transcendentals=0)


def dma(count):
    return pltpu.SemaphoreType.DMA((count,))


AMAX_PARTS = 4


def call(kernel, in_specs, out_specs, out_shape, name, scratch=(), flops=0, moved=1 << 20, mib=56, **more):
    return pl.pallas_call(
        kernel,
        in_specs=in_specs,
        out_specs=out_specs,
        out_shape=out_shape,
        scratch_shapes=list(scratch),
        compiler_params=params(mib),
        cost_estimate=cost(flops, moved),
        name=name,
        **more,
    )


def tie(arrays, mib=4):
    count = len(arrays)
    return call(
        tie_kernel,
        [HBM] * count,
        [HBM] * count,
        [shape(array.shape, array.dtype) for array in arrays],
        "tie",
        mib=mib,
        input_output_aliases={n: n for n in range(count)},
    )(*arrays)


def gate(arrays):
    return call(gate_kernel, [HBM] * len(arrays), VMEM, shape((8, 128), jnp.float32), "gate")(*arrays)


def on_device(inputs, preact, grad_act, weight):
    d, t = lax.axis_index("dp"), lax.axis_index("tensor")
    place = jnp.stack([d // 2, d % 2, t % 2]).astype(jnp.int32)
    tile = shape((8, 128), jnp.float32)

    first, second = call(
        slope_kernel,
        [HBM] * 2,
        [VMEM] * 2,
        [shape((HALF, FF_DEV))] * 2,
        "slope",
        [pltpu.VMEM((TOK_DEV, FF_DEV), jnp.bfloat16)] * 2 + [dma(2)],
    )(preact, grad_act)
    other_w = lax.ppermute(weight, "dp", CORE_SWAP)

    chunks = {0: first, 1: second}

    def step(steps, h, *after):
        at = [((sign * (steps - 1)) % NZ) * 2 + h for sign in (1, -1)]
        if after:
            held = tie([chunks[n] for n in at] + list(after))
            chunks.update(zip(at, held))
            after = held[2:]
        for sign, n in zip((1, -1), at):
            if steps == 4 and (sign, h) in ((-1, 0), (1, 1)):
                continue
            chunks[((sign * steps) % NZ) * 2 + h] = lax.ppermute(chunks[n], "dp", ring_perm(sign))
        return after

    def amax_part(part, before):
        return call(
            functools.partial(amax_kernel, part),
            [VMEM] * 4,
            VMEM,
            tile,
            "amax",
            flops=2 * TOK_DEV * FF_DEV * D // AMAX_PARTS,
            mib=8,
        )(before, inputs, first, second)

    step(1, 0)
    step(1, 1)
    amax = amax_part(0, jnp.zeros((8, 128), jnp.float32))
    (amax,) = step(2, 0, amax)
    amax = amax_part(1, amax)
    (amax,) = step(2, 1, amax)
    amax = amax_part(2, amax)
    (amax,) = step(3, 0, amax)
    amax = amax_part(3, amax)
    (amax,) = step(3, 1, amax)
    amax_other = lax.ppermute(amax, "dp", CORE_SWAP)
    step(4, 0)
    step(4, 1)

    block = call(
        block_kernel,
        [SMEM] + [HBM] * (NT + 2) + [VMEM] * 2,
        HBM,
        shape((NT, HALF, WIDE)),
        "block",
        [
            pltpu.VMEM((NT * HALF, FF_DEV), jnp.bfloat16),
            pltpu.VMEM((2, OWN, FF_DEV), jnp.bfloat16),
            pltpu.VMEM((NT, HALF, WIDE), jnp.bfloat16),
            dma(NT + 2),
            dma(2 * NZ),
        ],
        2 * 1024 * FF_DEV * CHIP,
        7 << 20,
    )(place, *[chunks[n] for n in range(NT)], weight, other_w, amax, amax_other)
    swapped = lax.all_to_all(block, "tensor", 0, 0)

    pieces = call(
        pick_kernel,
        [SMEM, HBM],
        [HBM] * NZ,
        [shape((HALF, CHIP))] * NZ,
        "pick",
        [pltpu.VMEM((HALF, D), jnp.bfloat16), pltpu.VMEM((NZ, HALF, CHIP), jnp.bfloat16), dma(NZ + 1)],
    )(place, inputs)
    come_in = {0: pieces[0]}
    for k in (1, 7, 2, 6, 3, 5, 4):
        come_in[k] = lax.ppermute(pieces[k], "dp", ring_perm(k))
    mine, here = call(
        stack_kernel,
        [HBM] * NZ,
        [VMEM] * 2,
        [shape((NZ, HALF, CHIP)), tile],
        "stack",
        [dma(NZ)],
    )(*[come_in[k] for k in range(NZ)])
    theirs = lax.ppermute(mine, "tensor", [(n, n ^ 1) for n in range(NT)])
    summed = call(sum_kernel, [VMEM] * 2, VMEM, shape((HALF, WIDE)), "sum", mib=16)(swapped, here)
    back = lax.ppermute(summed, ("dp", "tensor"), spread_perm(-1))

    copies, token = call(
        spread_kernel, [VMEM] * 2, [VMEM] * 2, [shape((NT, HALF, WIDE)), tile], "spread", mib=16
    )(back, here)
    whole = lax.all_to_all(copies, "tensor", 0, 0)
    own, other = call(
        outer_kernel,
        [SMEM, VMEM] + [VMEM] * (NT + 2),
        [VMEM] * 2,
        [shape((OWN, FF_DEV))] * 2,
        "outer",
        [pltpu.VMEM((NT * HALF, FF_DEV), jnp.bfloat16), pltpu.VMEM((NT * HALF, CHIP), jnp.bfloat16)],
        2 * 1024 * FF_DEV * CHIP,
        9 << 20,
        mib=48,
    )(place, token, *[chunks[n] for n in range(NT)], mine, theirs)
    come = lax.ppermute(other, "dp", CORE_SWAP)
    grad_input, weight_grad, grad_amax = call(
        final_kernel,
        [SMEM, HBM, HBM, HBM],
        [HBM, HBM, SMEM],
        [shape((TOK_DEV, D)), shape((OWN, FF_DEV), jnp.float32), shape((1, 1), jnp.float32)],
        "final",
        [
            pltpu.VMEM((NT, HALF, WIDE), jnp.bfloat16),
            pltpu.VMEM((TOK_DEV, D), jnp.bfloat16),
            pltpu.VMEM((OWN, FF_DEV), jnp.bfloat16),
            pltpu.VMEM((OWN, FF_DEV), jnp.bfloat16),
            pltpu.VMEM((OWN, FF_DEV), jnp.float32),
            dma(7),
        ],
    )(place, whole, own, come)
    return (grad_input, weight_grad, grad_amax.reshape(()))


def solution(mesh):
    placed = (P("dp", None), P("dp", "tensor"), P("dp", "tensor"), P("dp", "tensor"))
    return jax.shard_map(
        on_device,
        mesh=mesh,
        in_specs=placed,
        out_specs=(P("dp", None), P("dp", "tensor"), P()),
        check_vma=False,
    )
```

time: 363 us -> 145 us (0.40)
  blocking collectives: 130 us -> 0 us
  waiting for transfers between devices: 137 us -> 29.8 us
  starting transfers between devices: 0.12 us -> 67.9 us
  Pallas kernels: 0 us -> 31 us
  matrix products: 24.2 us -> 0 us
  other arithmetic: 24 us -> 0.56 us
  local copies, waits for them, and re-layouts: 29.7 us -> 11.9 us
  between operations: 14.5 us -> 1.48 us
    unnamed x4 -> x0, waiting for transfers between devices: 88.1 us -> none
    pmax x1 -> x0, blocking collectives: 80.6 us -> none  [shared_max(): return lax.pmax(local_max, ('dp', 'tensor'))]
    all_to_all x1 -> x0, blocking collectives: 49.5 us -> none  [on_device(): lax.all_to_all(summed, 'dp', split_axis=0, concat_axis=1, tiled=True)]
    psum x1 -> x0, waiting for transfers between devices: 48.3 us -> none  [on_device(): summed = lax.psum(block_part.astype(jnp.bfloat16), 'tensor')]
    ppermute x0 -> x26, starting transfers between devices: none -> 41.9 us  [the longest x14 22.5 us: step(): lax.ppermute(chunks[n], 'dp', ring_perm(sign))]
    pallas_call x0 -> x16, Pallas kernels: none -> 31 us  [the longest x1 7.53 us: on_device(): call(block_kernel, [SMEM] + [HBM] * (NT + 2) + [VMEM] * 2, HBM, shape((NT...]
    all_to_all x0 -> x2, starting transfers between devices: none -> 26 us  [the longest x1 18.9 us: on_device(): whole = lax.all_to_all(copies, 'tensor', 0, 0)]
    dot_general x2 -> x0, matrix products: 24.2 us -> none  [the longest x1 16.8 us: outer_rows(): lax.dot_general(left, right, (((0,), (0,)), ((), ())), preferred_element_...]
  transfers between devices with their start and end apart: 3 -> 28, of which waited for: 2 -> 8; matrix products, arithmetic and copies ran while one was open for 18% -> 0% of each run, Pallas kernels for 0% -> 13%
where the time goes in v2:
time: 145 us; the launch traced here: 143 us
  starting transfers between devices  67.9 us (47%)
  Pallas kernels  31 us (21%)
  waiting for transfers between devices  29.8 us (21%)
  local copies, waits for them, and re-layouts  11.9 us (8%)
  between operations  1.48 us (1%)
    ppermute x14, starting transfers between devices, step(): lax.ppermute(chunks[n], 'dp', ring_perm(sign))  22.5 us
    all_to_all x1, starting transfers between devices, on_device(): whole = lax.all_to_all(copies, 'tensor', 0, 0)  18.9 us
    ppermute x7, starting transfers between devices, on_device(): come_in[k] = lax.ppermute(pieces[k], 'dp', ring_perm(k))  16.6 us
    unnamed x96, local copies, waits for them, and re-layouts  11.9 us
    all_to_all x1, waiting for transfers between devices, on_device(): whole = lax.all_to_all(copies, 'tensor', 0, 0)  11.4 us
    ppermute x14, waiting for transfers between devices, step(): lax.ppermute(chunks[n], 'dp', ring_perm(sign))  8.56 us
    pallas_call x1, Pallas kernels, on_device(): call(block_kernel, [SMEM] + [HBM] * (NT + 2) + [VMEM] * 2, HBM, shape((NT...  7.53 us
    all_to_all x1, starting transfers between devices, on_device(): swapped = lax.all_to_all(block, 'tensor', 0, 0)  7.04 us
  transfers between devices with their start and end apart: 28, of which 8 were waited for; matrix products, arithmetic and copies ran while one was open for 0% of the time, Pallas kernels for 13%

profile of v2, /device:TPU:32, one launch (start us, length us, event | category | flops | bytes accessed | tf_op | source)
XLA Modules:
  0.0 142.5 jit_solution(11473328746805111180)
XLA Ops:
  0.6 0.1 collective-permute-start.14
  0.7 2.4 %slope.1 = (bf16[64,1536]{1,0:T(8,128)(2,1)}, bf16[64,1536]{1,0:T(8,128)(2,1)}) custom-call(bf16[128,1536]{1,0:T(8,128)(2,1)} %pre_hbm.1, bf16[128,1536]{1,0:T(8,128)(2,1)} %act_hbm.1), custom_call_target="tpu_custom_call" | custom-call | bytes 1048576 | tf_op jit(solution)/shard_map/slope/pallas_call | solution.py:298
  3.1 2.0 %collective-permute-start = (bf16[64,1536]{1,0:T(8,128)(2,1)}, bf16[64,1536]{1,0:T(8,128)(2,1)S(1)}, u32[]{:S(2)}, u32[]{:S(2)}) collective-permute-start(bf16[64,1536]{1,0:T(8,128)(2,1)} %get-tuple-element.34.first_ref.refs_1_.refs_0_), channel_id=1, source_target_pairs={{0,32},{16,240},{32,64},{48,16},{64,96},{80,48},{96,128},{112,80},... | collective-permute-start | bytes 589832 | tf_op jit(solution)/shard_map/ppermute | solution.py:319
  5.1 0.1 collective-permute-start.1
  5.2 1.9 %collective-permute-start.2 = (bf16[64,1536]{1,0:T(8,128)(2,1)}, bf16[64,1536]{1,0:T(8,128)(2,1)S(1)}, u32[]{:S(2)}, u32[]{:S(2)}) collective-permute-start(bf16[64,1536]{1,0:T(8,128)(2,1)} %get-tuple-element.35.second_ref.refs_2_.refs_1_), channel_id=1, source_target_pairs={{0,32},{16,240},{32,64},{48,16},{64,96},{80,48},{96,128},{112,80},... | collective-permute-start | bytes 589832 | tf_op jit(solution)/shard_map/ppermute | solution.py:319
  7.1 2.1 %collective-permute-start.3 = (bf16[64,1536]{1,0:T(8,128)(2,1)}, bf16[64,1536]{1,0:T(8,128)(2,1)S(1)}, u32[]{:S(2)}, u32[]{:S(2)}) collective-permute-start(bf16[64,1536]{1,0:T(8,128)(2,1)} %get-tuple-element.35.second_ref.refs_2_.refs_1_), channel_id=1, source_target_pairs={{0,224},{16,48},{32,0},{48,80},{64,32},{80,112},{96,64},{112,144},... | collective-permute-start | bytes 589832 | tf_op jit(solution)/shard_map/ppermute | solution.py:319
  9.2 1.4 copy-done
  10.6 0.9 copy-done.23
  11.6 0.9 copy-done.25
  12.5 1.5 %amax.4.refs_2_ = f32[8,128]{1,0:T(8,128)S(1)} custom-call(f32[8,128]{1,0:T(8,128)S(1)} %broadcast_in_dim.3.before_ref, bf16[128,6144]{1,0:T(8,128)(2,1)S(1)} %copy-done, bf16[64,1536]{1,0:T(8,128)(2,1)S(1)} %copy-done.23, bf16[64,1536]{1,0:T(8,128)(2,1)S(1)} %copy-done.25), custom_call_target="tpu_custom_call" | custom-call | flops 603979776 | bytes 1048576 | tf_op jit(solution)/shard_map/amax/pallas_call | solution.py:323
  14.1 1.7 %collective-permute-start.4 = (bf16[64,1536]{1,0:T(8,128)(2,1)S(1)}, bf16[64,1536]{1,0:T(8,128)(2,1)S(1)}, u32[]{:S(2)}, u32[]{:S(2)}) collective-permute-start(bf16[64,1536]{1,0:T(8,128)(2,1)S(1)} %get-tuple-element.36.refs_3_.refs_2_), channel_id=1, source_target_pairs={{0,32},{16,240},{32,64},{48,16},{64,96},{80,48},{96,128},{112,80},... | collective-permute-start | bytes 589832 | tf_op jit(solution)/shard_map/ppermute | solution.py:319
  15.7 1.7 %collective-permute-start.5 = (bf16[64,1536]{1,0:T(8,128)(2,1)S(1)}, bf16[64,1536]{1,0:T(8,128)(2,1)S(1)}, u32[]{:S(2)}, u32[]{:S(2)}) collective-permute-start(bf16[64,1536]{1,0:T(8,128)(2,1)S(1)} %get-tuple-element.39.refs_15_.refs_14_), channel_id=1, source_target_pairs={{0,224},{16,48},{32,0},{48,80},{64,32},{80,112},{96,64},{112,144},... | collective-permute-start | bytes 589832 | tf_op jit(solution)/shard_map/ppermute | solution.py:319
  17.5 1.5 %amax.5.refs_2_ = f32[8,128]{1,0:T(8,128)S(1)} custom-call(f32[8,128]{1,0:T(8,128)S(1)} %get-tuple-element.37.before_ref, bf16[128,6144]{1,0:T(8,128)(2,1)S(1)} %copy-done.1, bf16[64,1536]{1,0:T(8,128)(2,1)S(1)} %copy-done.23, bf16[64,1536]{1,0:T(8,128)(2,1)S(1)} %copy-done.25), custom_call_target="tpu_custom_call" | custom-call | flops 603979776 | bytes 1048576 | tf_op jit(solution)/shard_map/amax/pallas_call | solution.py:323
  19.0 0.0 collective-permute-done.2.refs_0_
  19.1 0.0 collective-permute-done.3.refs_1_
  19.1 1.3 collective-permute-start.6
  20.3 2.1 %collective-permute-start.7 = (bf16[64,1536]{1,0:T(8,128)(2,1)S(1)}, bf16[64,1536]{1,0:T(8,128)(2,1)S(1)}, u32[]{:S(2)}, u32[]{:S(2)}) collective-permute-start(bf16[64,1536]{1,0:T(8,128)(2,1)S(1)} %get-tuple-element.42.refs_16_.refs_15_), channel_id=1, source_target_pairs={{0,224},{16,48},{32,0},{48,80},{64,32},{80,112},{96,64},{112,144},... | collective-permute-start | bytes 589832 | tf_op jit(solution)/shard_map/ppermute | solution.py:319
  22.4 1.5 %amax.6.refs_2_ = f32[8,128]{1,0:T(8,128)S(1)} custom-call(f32[8,128]{1,0:T(8,128)S(1)} %get-tuple-element.40.before_ref, bf16[128,6144]{1,0:T(8,128)(2,1)S(1)} %copy-done.1, bf16[64,1536]{1,0:T(8,128)(2,1)S(1)} %copy-done.23, bf16[64,1536]{1,0:T(8,128)(2,1)S(1)} %copy-done.25), custom_call_target="tpu_custom_call" | custom-call | flops 603979776 | bytes 1048576 | tf_op jit(solution)/shard_map/amax/pallas_call | solution.py:323
  24.0 3.1 %collective-permute-start.8 = (bf16[64,1536]{1,0:T(8,128)(2,1)S(1)}, bf16[64,1536]{1,0:T(8,128)(2,1)S(1)}, u32[]{:S(2)}, u32[]{:S(2)}) collective-permute-start(bf16[64,1536]{1,0:T(8,128)(2,1)S(1)} %get-tuple-element.41.refs_5_.refs_4_), channel_id=1, source_target_pairs={{0,32},{16,240},{32,64},{48,16},{64,96},{80,48},{96,128},{112,80},... | collective-permute-start | bytes 589832 | tf_op jit(solution)/shard_map/ppermute | solution.py:319
  27.1 1.5 %amax.7.refs_2_ = f32[8,128]{1,0:T(8,128)S(1)} custom-call(f32[8,128]{1,0:T(8,128)S(1)} %get-tuple-element.43.before_ref, bf16[128,6144]{1,0:T(8,128)(2,1)S(1)} %copy-done.1, bf16[64,1536]{1,0:T(8,128)(2,1)S(1)} %copy-done.23, bf16[64,1536]{1,0:T(8,128)(2,1)S(1)} %copy-done.25), custom_call_target="tpu_custom_call" | custom-call | flops 603979776 | bytes 1048576 | tf_op jit(solution)/shard_map/amax/pallas_call | solution.py:323
  28.8 0.0 copy-start.21
  28.8 1.9 %collective-permute-start.11 = (bf16[64,1536]{1,0:T(8,128)(2,1)S(1)}, bf16[64,1536]{1,0:T(8,128)(2,1)S(1)}, u32[]{:S(2)}, u32[]{:S(2)}) collective-permute-start(bf16[64,1536]{1,0:T(8,128)(2,1)S(1)} %get-tuple-element.45.refs_14_.refs_13_), channel_id=1, source_target_pairs={{0,224},{16,48},{32,0},{48,80},{64,32},{80,112},{96,64},{112,144},... | collective-permute-start | bytes 589832 | tf_op jit(solution)/shard_map/ppermute | solution.py:319
  30.7 1.6 %collective-permute-start.9 = (bf16[64,1536]{1,0:T(8,128)(2,1)S(1)}, bf16[64,1536]{1,0:T(8,128)(2,1)S(1)}, u32[]{:S(2)}, u32[]{:S(2)}) collective-permute-start(bf16[64,1536]{1,0:T(8,128)(2,1)S(1)} %get-tuple-element.44.refs_6_.refs_5_), channel_id=1, source_target_pairs={{0,32},{16,240},{32,64},{48,16},{64,96},{80,48},{96,128},{112,80},... | collective-permute-start | bytes 589832 | tf_op jit(solution)/shard_map/ppermute | solution.py:319
  32.3 1.4 collective-permute-start.13
  33.7 1.7 %collective-permute-start.10 = (bf16[64,1536]{1,0:T(8,128)(2,1)S(1)}, bf16[64,1536]{1,0:T(8,128)(2,1)S(1)}, u32[]{:S(2)}, u32[]{:S(2)}) collective-permute-start(bf16[64,1536]{1,0:T(8,128)(2,1)S(1)} %collective-permute-done.8.refs_7_.refs_6_), channel_id=1, source_target_pairs={{0,32},{16,240},{32,64},{48,16},{64,96},{80,48},{96,128},{112,80},... | collective-permute-start | bytes 589832 | tf_op jit(solution)/shard_map/ppermute | solution.py:319
  35.3 2.4 %collective-permute-done.11.refs_12_.refs_11_ = bf16[64,1536]{1,0:T(8,128)(2,1)S(1)} collective-permute-done((bf16[64,1536]{1,0:T(8,128)(2,1)S(1)}, bf16[64,1536]{1,0:T(8,128)(2,1)S(1)}, u32[]{:S(2)}, u32[]{:S(2)}) %collective-permute-start.11) | collective-permute-done | bytes 196640 | tf_op jit(solution)/shard_map/ppermute | solution.py:319
  37.8 0.6 pad_add_fusion.refs_0_.at_ref
  38.3 3.6 %collective-permute-done.13.refs_11_.refs_10_ = bf16[64,1536]{1,0:T(8,128)(2,1)S(1)} collective-permute-done((bf16[64,1536]{1,0:T(8,128)(2,1)S(1)}, bf16[64,1536]{1,0:T(8,128)(2,1)S(1)}, u32[]{:S(2)}, u32[]{:S(2)}) %collective-permute-start.13) | collective-permute-done | bytes 196640 | tf_op jit(solution)/shard_map/ppermute | solution.py:319
  42.0 2.5 %collective-permute-done.12.refs_10_.refs_9_ = bf16[64,1536]{1,0:T(8,128)(2,1)S(1)} collective-permute-done((bf16[64,1536]{1,0:T(8,128)(2,1)S(1)}, bf16[64,1536]{1,0:T(8,128)(2,1)S(1)}, u32[]{:S(2)}, u32[]{:S(2)}) %collective-permute-start.12) | collective-permute-done | bytes 196640 | tf_op jit(solution)/shard_map/ppermute | solution.py:319
  44.6 0.6 copy-done.37
  45.1 7.5 %block.1 = bf16[16,64,896]{2,1,0:T(8,128)(2,1)} custom-call(s32[3]{0:T(128)} %pad_add_fusion.refs_0_.at_ref, bf16[64,1536]{1,0:T(8,128)(2,1)} %get-tuple-element.34.first_ref.refs_1_.refs_0_, bf16[64,1536]{1,0:T(8,128)(2,1)} %get-tuple-element.35.second_ref.refs_2_.refs_1_, bf16[64,1536]{1,0:T(8,128)(2,1)} %copy-done.15, bf16[64,1536]{1,0:T(8,128)(2,1)} %copy-done.3, ...), custom_call_target="tpu_custom_call" | custom-call | flops 2415919104 | bytes 7340032 | tf_op jit(solution)/shard_map/block/pallas_call | solution.py:347
  52.7 7.0 %all-to-all-start = ((bf16[16,64,896]{2,1,0:T(8,128)(2,1)}), bf16[16,64,896]{2,1,0:T(8,128)(2,1)S(1)}, u32[]{:S(2)}, u32[]{:S(2)}) async-start(bf16[16,64,896]{2,1,0:T(8,128)(2,1)} %block.1), calls=%async_computation | async-start | bytes 3670016 | tf_op jit(solution)/shard_map/all_to_all | solution.py:363
  59.7 2.8 %pick.1 = (bf16[64,768]{1,0:T(8,128)(2,1)}, bf16[64,768]{1,0:T(8,128)(2,1)}, bf16[64,768]{1,0:T(8,128)(2,1)}, bf16[64,768]{1,0:T(8,128)(2,1)}, bf16[64,768]{1,0:...) custom-call(s32[3]{0:T(128)} %pad_add_fusion.refs_0_.at_ref, ...), custom_call_target="tpu_custom_call" | custom-call | bytes 1048576 | tf_op jit(solution)/shard_map/pick/pallas_call | solution.py:365
  62.5 3.3 %collective-permute-start.16 = (bf16[64,768]{1,0:T(8,128)(2,1)}, bf16[64,768]{1,0:T(8,128)(2,1)S(1)}, u32[]{:S(2)}, u32[]{:S(2)}) collective-permute-start(bf16[64,768]{1,0:T(8,128)(2,1)} %get-tuple-element.49), channel_id=1, source_target_pairs={{0,32},{16,240},{32,64},{48,16},{64,96},{80,48},{96,128},{112,80},... | collective-permute-start | bytes 294920 | tf_op jit(solution)/shard_map/ppermute | solution.py:375
  65.8 3.0 %collective-permute-start.17 = (bf16[64,768]{1,0:T(8,128)(2,1)}, bf16[64,768]{1,0:T(8,128)(2,1)S(1)}, u32[]{:S(2)}, u32[]{:S(2)}) collective-permute-start(bf16[64,768]{1,0:T(8,128)(2,1)} %get-tuple-element.50), channel_id=1, source_target_pairs={{0,64},{16,208},{32,96},{48,240},{64,128},{80,16},{96,160},{112,48... | collective-permute-start | bytes 294920 | tf_op jit(solution)/shard_map/ppermute | solution.py:375
  68.8 6.1 %collective-permute-start.19 = (bf16[64,768]{1,0:T(8,128)(2,1)}, bf16[64,768]{1,0:T(8,128)(2,1)S(1)}, u32[]{:S(2)}, u32[]{:S(2)}) collective-permute-start(bf16[64,768]{1,0:T(8,128)(2,1)} %get-tuple-element.52), channel_id=1, source_target_pairs={{0,128},{16,144},{32,160},{48,176},{64,192},{80,208},{96,224},{112... | collective-permute-start | bytes 294920 | tf_op jit(solution)/shard_map/ppermute | solution.py:375
  75.0 0.0 collective-permute-start.20
  75.0 1.5 %collective-permute-start.21 = (bf16[64,768]{1,0:T(8,128)(2,1)}, bf16[64,768]{1,0:T(8,128)(2,1)S(1)}, u32[]{:S(2)}, u32[]{:S(2)}) collective-permute-start(bf16[64,768]{1,0:T(8,128)(2,1)} %get-tuple-element.54), channel_id=1, source_target_pairs={{0,192},{16,80},{32,224},{48,112},{64,0},{80,144},{96,32},{112,176... | collective-permute-start | bytes 294920 | tf_op jit(solution)/shard_map/ppermute | solution.py:375
  76.4 2.7 %collective-permute-start.22 = (bf16[64,768]{1,0:T(8,128)(2,1)}, bf16[64,768]{1,0:T(8,128)(2,1)S(1)}, u32[]{:S(2)}, u32[]{:S(2)}) collective-permute-start(bf16[64,768]{1,0:T(8,128)(2,1)} %get-tuple-element.55), channel_id=1, source_target_pairs={{0,224},{16,48},{32,0},{48,80},{64,32},{80,112},{96,64},{112,144},... | collective-permute-start | bytes 294920 | tf_op jit(solution)/shard_map/ppermute | solution.py:375
  79.1 1.0 collective-permute-done.18.refs_3_
  80.1 1.6 %collective-permute-done.19.refs_4_ = bf16[64,768]{1,0:T(8,128)(2,1)S(1)} collective-permute-done((bf16[64,768]{1,0:T(8,128)(2,1)}, bf16[64,768]{1,0:T(8,128)(2,1)S(1)}, u32[]{:S(2)}, u32[]{:S(2)}) %collective-permute-start.19) | collective-permute-done | bytes 98336 | tf_op jit(solution)/shard_map/ppermute | solution.py:375
  81.7 4.2 %collective-permute-done.20.refs_5_ = bf16[64,768]{1,0:T(8,128)(2,1)S(1)} collective-permute-done((bf16[64,768]{1,0:T(8,128)(2,1)}, bf16[64,768]{1,0:T(8,128)(2,1)S(1)}, u32[]{:S(2)}, u32[]{:S(2)}) %collective-permute-start.20) | collective-permute-done | bytes 98336 | tf_op jit(solution)/shard_map/ppermute | solution.py:375
  85.9 0.6 copy-done.44
  86.5 0.0 copy-done.45
  86.5 0.1 copy-done.46
  86.6 2.2 %stack.17 = (bf16[8,64,768]{2,1,0:T(8,128)(2,1)}, f32[8,128]{1,0:T(8,128)}) custom-call(bf16[64,768]{1,0:T(8,128)(2,1)} %get-tuple-element.48.refs_0_, bf16[64,768]{1,0:T(8,128)(2,1)} %copy-done.40, bf16[64,768]{1,0:T(8,128)(2,1)} %copy-done.41, bf16[64,768]{1,0:T(8,128)(2,1)} %copy-done.42, bf16[64,768]{1,0:T(8,128)(2,1)} %copy-done.43, ...), custom_call_target="tpu_custom_call" | custom-call | bytes 1048576 | tf_op jit(solution)/shard_map/stack/pallas_call | solution.py:376
  88.7 2.0 %collective-permute-start.24 = (bf16[8,64,768]{2,1,0:T(8,128)(2,1)}, bf16[8,64,768]{2,1,0:T(8,128)(2,1)S(1)}, u32[]{:S(2)}, u32[]{:S(2)}) collective-permute-start(bf16[8,64,768]{2,1,0:T(8,128)(2,1)} %get-tuple-element.59.refs_16_), channel_id=1, source_target_pairs={{0,1},{1,0},{2,3},{3,2},{4,5},{5,4},{6,7},{7,6},{8,9},{9,8},{10,11... | collective-permute-start | bytes 2359304 | tf_op jit(solution)/shard_map/ppermute | solution.py:384
  90.7 0.7 copy-done.19
  91.4 0.2 sum.1
  91.6 0.7 collective-permute-start.23
  92.3 1.4 spread.1
  93.7 0.0 copy-start.22
  93.8 18.9 %all-to-all-start.1 = ((bf16[16,64,896]{2,1,0:T(8,128)(2,1)}), bf16[16,64,896]{2,1,0:T(8,128)(2,1)}, u32[]{:S(2)}, u32[]{:S(2)}) async-start(bf16[16,64,896]{2,1,0:T(8,128)(2,1)} %get-tuple-element.57), calls=%async_computation.1 | async-start | bytes 3670016 | tf_op jit(solution)/shard_map/all_to_all | solution.py:391
  112.8 0.9 copy-done.28
  113.7 0.9 copy-done.30
  114.7 0.9 copy-done.32
  115.6 0.9 copy-done.34
  116.5 0.9 copy-done.36
  117.4 0.9 copy-done.38
  118.4 3.5 %outer.1 = (bf16[384,1536]{1,0:T(8,128)(2,1)S(1)}, bf16[384,1536]{1,0:T(8,128)(2,1)}) custom-call(s32[3]{0:T(128)S(1)} %copy-done.20, f32[8,128]{1,0:T(8,128)S(1)} %get-tuple-element.58._, bf16[64,1536]{1,0:T(8,128)(2,1)S(1)} %copy-done.24, bf16[64,1536]{1,0:T(8,128)(2,1)S(1)} %copy-done.26, bf16[64,1536]{1,0:T(8,128)(2,1)S(1)} %copy-done.16, ...), custom_call_target="tpu_custom_call" | custom-call | flops 2415919104 | bytes 9437184 | tf_op jit(solution)/shard_map/outer/pallas_call | solution.py:392
  121.9 1.0 copy-done.2
  122.9 3.1 %collective-permute-done.25.come_hbm = bf16[384,1536]{1,0:T(8,128)(2,1)S(1)} collective-permute-done((bf16[384,1536]{1,0:T(8,128)(2,1)}, bf16[384,1536]{1,0:T(8,128)(2,1)S(1)}, u32[]{:S(2)}, u32[]{:S(2)}) %collective-permute-start.25) | collective-permute-done | bytes 1179680 | tf_op jit(solution)/shard_map/ppermute | solution.py:403
  126.0 11.4 %all-to-all-done.1.whole_hbm = bf16[16,64,896]{2,1,0:T(8,128)(2,1)} async-done(((bf16[16,64,896]{2,1,0:T(8,128)(2,1)}), bf16[16,64,896]{2,1,0:T(8,128)(2,1)}, u32[]{:S(2)}, u32[]{:S(2)}) %all-to-all-start.1) | async-done | bytes 1835040 | tf_op jit(solution)/shard_map/all_to_all | solution.py:391
  137.4 5.0 %final.1 = (bf16[128,6144]{1,0:T(8,128)(2,1)}, f32[384,1536]{1,0:T(8,128)}, f32[1,1]{1,0:T(1,128)}) custom-call(s32[3]{0:T(128)} %pad_add_fusion.refs_0_.at_ref, bf16[16,64,896]{2,1,0:T(8,128)(2,1)} %all-to-all-done.1.whole_hbm, bf16[384,1536]{1,0:T(8,128)(2,1)} %copy-done.2, bf16[384,1536]{1,0:T(8,128)(2,1)} %copy-done.39), custom_call_target="tpu_custom_call" | custom-call | bytes 1048576 | tf_op jit(solution)/shard_map/final/pallas_call | solution.py:404
  (106 shorter events, 0.2 us)
Async XLA Ops:
  0.6 43.8 %collective-permute-start.14 = (bf16[384,1536]{1,0:T(8,128)(2,1)}, bf16[384,1536]{1,0:T(8,128)(2,1)}, u32[]{:S(2)}, u32[]{:S(2)}) collective-permute-start(bf16[384,1536]{1,0:T(8,128)(2,1)} %refs_17_.1), channel_id=1, source_target_pairs={{0,16},{16,0},{32,48},{48,32},{64,80},{80,64},{96,112},{112,96},{1... | collective-permute-start | bytes 3538952 | tf_op jit(solution)/shard_map/ppermute | solution.py:306
  3.1 10.9 %collective-permute-start = (bf16[64,1536]{1,0:T(8,128)(2,1)}, bf16[64,1536]{1,0:T(8,128)(2,1)S(1)}, u32[]{:S(2)}, u32[]{:S(2)}) collective-permute-start(bf16[64,1536]{1,0:T(8,128)(2,1)} %get-tuple-element.34.first_ref.refs_1_.refs_0_), channel_id=1, source_target_pairs={{0,32},{16,240},{32,64},{48,16},{64,96},{80,48},{96,128},{112,80},... | collective-permute-start | bytes 589832 | tf_op jit(solution)/shard_map/ppermute | solution.py:319
  5.1 9.0 %collective-permute-start.1 = (bf16[64,1536]{1,0:T(8,128)(2,1)}, bf16[64,1536]{1,0:T(8,128)(2,1)S(1)}, u32[]{:S(2)}, u32[]{:S(2)}) collective-permute-start(bf16[64,1536]{1,0:T(8,128)(2,1)} %get-tuple-element.34.first_ref.refs_1_.refs_0_), channel_id=1, source_target_pairs={{0,224},{16,48},{32,0},{48,80},{64,32},{80,112},{96,64},{112,144},... | collective-permute-start | bytes 589832 | tf_op jit(solution)/shard_map/ppermute | solution.py:319
  5.2 13.8 %collective-permute-start.2 = (bf16[64,1536]{1,0:T(8,128)(2,1)}, bf16[64,1536]{1,0:T(8,128)(2,1)S(1)}, u32[]{:S(2)}, u32[]{:S(2)}) collective-permute-start(bf16[64,1536]{1,0:T(8,128)(2,1)} %get-tuple-element.35.second_ref.refs_2_.refs_1_), channel_id=1, source_target_pairs={{0,32},{16,240},{32,64},{48,16},{64,96},{80,48},{96,128},{112,80},... | collective-permute-start | bytes 589832 | tf_op jit(solution)/shard_map/ppermute | solution.py:319
  7.1 11.9 %collective-permute-start.3 = (bf16[64,1536]{1,0:T(8,128)(2,1)}, bf16[64,1536]{1,0:T(8,128)(2,1)S(1)}, u32[]{:S(2)}, u32[]{:S(2)}) collective-permute-start(bf16[64,1536]{1,0:T(8,128)(2,1)} %get-tuple-element.35.second_ref.refs_2_.refs_1_), channel_id=1, source_target_pairs={{0,224},{16,48},{32,0},{48,80},{64,32},{80,112},{96,64},{112,144},... | collective-permute-start | bytes 589832 | tf_op jit(solution)/shard_map/ppermute | solution.py:319
  9.2 1.4 copy-start
  12.5 5.0 %copy-start.1 = (bf16[128,6144]{1,0:T(8,128)(2,1)S(1)}, bf16[128,6144]{1,0:T(8,128)(2,1)}, u32[]{:S(2)}) copy-start(bf16[128,6144]{1,0:T(8,128)(2,1)} %in_hbm.1) | copy-start | bytes 4718596
  14.1 9.9 %copy-start.15 = (bf16[64,1536]{1,0:T(8,128)(2,1)}, bf16[64,1536]{1,0:T(8,128)(2,1)S(1)}, u32[]{:S(2)}) copy-start(bf16[64,1536]{1,0:T(8,128)(2,1)S(1)} %get-tuple-element.36.refs_3_.refs_2_) | copy-start | bytes 589828
  14.1 9.9 %copy-start.17 = (bf16[64,1536]{1,0:T(8,128)(2,1)}, bf16[64,1536]{1,0:T(8,128)(2,1)S(1)}, u32[]{:S(2)}) copy-start(bf16[64,1536]{1,0:T(8,128)(2,1)S(1)} %get-tuple-element.39.refs_15_.refs_14_) | copy-start | bytes 589828
  14.1 9.9 %collective-permute-start.4 = (bf16[64,1536]{1,0:T(8,128)(2,1)S(1)}, bf16[64,1536]{1,0:T(8,128)(2,1)S(1)}, u32[]{:S(2)}, u32[]{:S(2)}) collective-permute-start(bf16[64,1536]{1,0:T(8,128)(2,1)S(1)} %get-tuple-element.36.refs_3_.refs_2_), channel_id=1, source_target_pairs={{0,32},{16,240},{32,64},{48,16},{64,96},{80,48},{96,128},{112,80},... | collective-permute-start | bytes 589832 | tf_op jit(solution)/shard_map/ppermute | solution.py:319
  15.7 8.2 %collective-permute-start.5 = (bf16[64,1536]{1,0:T(8,128)(2,1)S(1)}, bf16[64,1536]{1,0:T(8,128)(2,1)S(1)}, u32[]{:S(2)}, u32[]{:S(2)}) collective-permute-start(bf16[64,1536]{1,0:T(8,128)(2,1)S(1)} %get-tuple-element.39.refs_15_.refs_14_), channel_id=1, source_target_pairs={{0,224},{16,48},{32,0},{48,80},{64,32},{80,112},{96,64},{112,144},... | collective-permute-start | bytes 589832 | tf_op jit(solution)/shard_map/ppermute | solution.py:319
  19.1 9.6 %copy-start.3 = (bf16[64,1536]{1,0:T(8,128)(2,1)}, bf16[64,1536]{1,0:T(8,128)(2,1)S(1)}, u32[]{:S(2)}) copy-start(bf16[64,1536]{1,0:T(8,128)(2,1)S(1)} %get-tuple-element.38.refs_4_.refs_3_) | copy-start | bytes 589828
  19.1 9.6 %copy-start.7 = (bf16[64,1536]{1,0:T(8,128)(2,1)}, bf16[64,1536]{1,0:T(8,128)(2,1)S(1)}, u32[]{:S(2)}) copy-start(bf16[64,1536]{1,0:T(8,128)(2,1)S(1)} %get-tuple-element.42.refs_16_.refs_15_) | copy-start | bytes 589828
  19.1 9.6 %collective-permute-start.6 = (bf16[64,1536]{1,0:T(8,128)(2,1)S(1)}, bf16[64,1536]{1,0:T(8,128)(2,1)S(1)}, u32[]{:S(2)}, u32[]{:S(2)}) collective-permute-start(bf16[64,1536]{1,0:T(8,128)(2,1)S(1)} %get-tuple-element.38.refs_4_.refs_3_), channel_id=1, source_target_pairs={{0,32},{16,240},{32,64},{48,16},{64,96},{80,48},{96,128},{112,80},... | collective-permute-start | bytes 589832 | tf_op jit(solution)/shard_map/ppermute | solution.py:319
  20.3 8.4 %collective-permute-start.7 = (bf16[64,1536]{1,0:T(8,128)(2,1)S(1)}, bf16[64,1536]{1,0:T(8,128)(2,1)S(1)}, u32[]{:S(2)}, u32[]{:S(2)}) collective-permute-start(bf16[64,1536]{1,0:T(8,128)(2,1)S(1)} %get-tuple-element.42.refs_16_.refs_15_), channel_id=1, source_target_pairs={{0,224},{16,48},{32,0},{48,80},{64,32},{80,112},{96,64},{112,144},... | collective-permute-start | bytes 589832 | tf_op jit(solution)/shard_map/ppermute | solution.py:319
  24.0 20.5 %copy-start.5 = (bf16[64,1536]{1,0:T(8,128)(2,1)}, bf16[64,1536]{1,0:T(8,128)(2,1)S(1)}, u32[]{:S(2)}) copy-start(bf16[64,1536]{1,0:T(8,128)(2,1)S(1)} %get-tuple-element.41.refs_5_.refs_4_) | copy-start | bytes 589828
  24.0 20.5 %copy-start.9 = (bf16[64,1536]{1,0:T(8,128)(2,1)}, bf16[64,1536]{1,0:T(8,128)(2,1)S(1)}, u32[]{:S(2)}) copy-start(bf16[64,1536]{1,0:T(8,128)(2,1)S(1)} %get-tuple-element.46.refs_13_.refs_12_) | copy-start | bytes 589828
  24.0 9.7 %collective-permute-start.8 = (bf16[64,1536]{1,0:T(8,128)(2,1)S(1)}, bf16[64,1536]{1,0:T(8,128)(2,1)S(1)}, u32[]{:S(2)}, u32[]{:S(2)}) collective-permute-start(bf16[64,1536]{1,0:T(8,128)(2,1)S(1)} %get-tuple-element.41.refs_5_.refs_4_), channel_id=1, source_target_pairs={{0,32},{16,240},{32,64},{48,16},{64,96},{80,48},{96,128},{112,80},... | collective-permute-start | bytes 589832 | tf_op jit(solution)/shard_map/ppermute | solution.py:319
  28.7 15.7 %copy-start.11 = (bf16[64,1536]{1,0:T(8,128)(2,1)}, bf16[64,1536]{1,0:T(8,128)(2,1)S(1)}, u32[]{:S(2)}) copy-start(bf16[64,1536]{1,0:T(8,128)(2,1)S(1)} %get-tuple-element.44.refs_6_.refs_5_) | copy-start | bytes 589828
  28.7 15.7 %copy-start.13 = (bf16[64,1536]{1,0:T(8,128)(2,1)}, bf16[64,1536]{1,0:T(8,128)(2,1)S(1)}, u32[]{:S(2)}) copy-start(bf16[64,1536]{1,0:T(8,128)(2,1)S(1)} %get-tuple-element.45.refs_14_.refs_13_) | copy-start | bytes 589828
  28.8 15.7 %copy-start.21 = (f32[8,128]{1,0:T(8,128)}, f32[8,128]{1,0:T(8,128)S(1)}, u32[]{:S(2)}) copy-start(f32[8,128]{1,0:T(8,128)S(1)} %get-tuple-element.47.refs_19_) | copy-start | bytes 12292
  28.8 9.0 %collective-permute-start.11 = (bf16[64,1536]{1,0:T(8,128)(2,1)S(1)}, bf16[64,1536]{1,0:T(8,128)(2,1)S(1)}, u32[]{:S(2)}, u32[]{:S(2)}) collective-permute-start(bf16[64,1536]{1,0:T(8,128)(2,1)S(1)} %get-tuple-element.45.refs_14_.refs_13_), channel_id=1, source_target_pairs={{0,224},{16,48},{32,0},{48,80},{64,32},{80,112},{96,64},{112,144},... | collective-permute-start | bytes 589832 | tf_op jit(solution)/shard_map/ppermute | solution.py:319
  30.7 1.6 %collective-permute-start.15 = (f32[8,128]{1,0:T(8,128)S(1)}, f32[8,128]{1,0:T(8,128)S(1)}, u32[]{:S(2)}, u32[]{:S(2)}) collective-permute-start(f32[8,128]{1,0:T(8,128)S(1)} %get-tuple-element.47.refs_19_), channel_id=1, source_target_pairs={{0,16},{16,0},{32,48},{48,32},{64,80},{80,64},{96,112},{112,96},{1... | collective-permute-start | bytes 12296 | tf_op jit(solution)/shard_map/ppermute | solution.py:343
  30.7 7.6 %collective-permute-start.9 = (bf16[64,1536]{1,0:T(8,128)(2,1)S(1)}, bf16[64,1536]{1,0:T(8,128)(2,1)S(1)}, u32[]{:S(2)}, u32[]{:S(2)}) collective-permute-start(bf16[64,1536]{1,0:T(8,128)(2,1)S(1)} %get-tuple-element.44.refs_6_.refs_5_), channel_id=1, source_target_pairs={{0,32},{16,240},{32,64},{48,16},{64,96},{80,48},{96,128},{112,80},... | collective-permute-start | bytes 589832 | tf_op jit(solution)/shard_map/ppermute | solution.py:319
  32.3 12.2 %copy-start.47 = (f32[8,128]{1,0:T(8,128)}, f32[8,128]{1,0:T(8,128)S(1)}, u32[]{:S(2)}) copy-start(f32[8,128]{1,0:T(8,128)S(1)} %collective-permute-done.15.refs_20_) | copy-start | bytes 12292
  32.3 9.6 %collective-permute-start.13 = (bf16[64,1536]{1,0:T(8,128)(2,1)S(1)}, bf16[64,1536]{1,0:T(8,128)(2,1)S(1)}, u32[]{:S(2)}, u32[]{:S(2)}) collective-permute-start(bf16[64,1536]{1,0:T(8,128)(2,1)S(1)} %get-tuple-element.46.refs_13_.refs_12_), channel_id=1, source_target_pairs={{0,224},{16,48},{32,0},{48,80},{64,32},{80,112},{96,64},{112,144},... | collective-permute-start | bytes 589832 | tf_op jit(solution)/shard_map/ppermute | solution.py:319
  33.7 10.8 %copy-start.27 = (bf16[64,1536]{1,0:T(8,128)(2,1)}, bf16[64,1536]{1,0:T(8,128)(2,1)S(1)}, u32[]{:S(2)}) copy-start(bf16[64,1536]{1,0:T(8,128)(2,1)S(1)} %collective-permute-done.8.refs_7_.refs_6_) | copy-start | bytes 589828
  33.7 8.3 %collective-permute-start.10 = (bf16[64,1536]{1,0:T(8,128)(2,1)S(1)}, bf16[64,1536]{1,0:T(8,128)(2,1)S(1)}, u32[]{:S(2)}, u32[]{:S(2)}) collective-permute-start(bf16[64,1536]{1,0:T(8,128)(2,1)S(1)} %collective-permute-done.8.refs_7_.refs_6_), channel_id=1, source_target_pairs={{0,32},{16,240},{32,64},{48,16},{64,96},{80,48},{96,128},{112,80},... | collective-permute-start | bytes 589832 | tf_op jit(solution)/shard_map/ppermute | solution.py:319
  37.8 6.8 %copy-start.29 = (bf16[64,1536]{1,0:T(8,128)(2,1)}, bf16[64,1536]{1,0:T(8,128)(2,1)S(1)}, u32[]{:S(2)}) copy-start(bf16[64,1536]{1,0:T(8,128)(2,1)S(1)} %collective-permute-done.11.refs_12_.refs_11_) | copy-start | bytes 589828
  37.8 6.7 %collective-permute-start.12 = (bf16[64,1536]{1,0:T(8,128)(2,1)S(1)}, bf16[64,1536]{1,0:T(8,128)(2,1)S(1)}, u32[]{:S(2)}, u32[]{:S(2)}) collective-permute-start(bf16[64,1536]{1,0:T(8,128)(2,1)S(1)} %collective-permute-done.11.refs_12_.refs_11_), channel_id=1, source_target_pairs={{0,224},{16,48},{32,0},{48,80},{64,32},{80,112},{96,64},{112,144},... | collective-permute-start | bytes 589832 | tf_op jit(solution)/shard_map/ppermute | solution.py:319
  38.3 6.2 %copy-start.31 = (bf16[64,1536]{1,0:T(8,128)(2,1)}, bf16[64,1536]{1,0:T(8,128)(2,1)S(1)}, u32[]{:S(2)}) copy-start(bf16[64,1536]{1,0:T(8,128)(2,1)S(1)} %collective-permute-done.9.refs_8_.refs_7_) | copy-start | bytes 589828
  42.0 2.6 %copy-start.33 = (bf16[64,1536]{1,0:T(8,128)(2,1)}, bf16[64,1536]{1,0:T(8,128)(2,1)S(1)}, u32[]{:S(2)}) copy-start(bf16[64,1536]{1,0:T(8,128)(2,1)S(1)} %collective-permute-done.13.refs_11_.refs_10_) | copy-start | bytes 589828
  42.0 2.6 %copy-start.35 = (bf16[64,1536]{1,0:T(8,128)(2,1)}, bf16[64,1536]{1,0:T(8,128)(2,1)S(1)}, u32[]{:S(2)}) copy-start(bf16[64,1536]{1,0:T(8,128)(2,1)S(1)} %collective-permute-done.10.refs_9_.refs_8_) | copy-start | bytes 589828
  52.7 38.0 %all-to-all-start = ((bf16[16,64,896]{2,1,0:T(8,128)(2,1)}), bf16[16,64,896]{2,1,0:T(8,128)(2,1)S(1)}, u32[]{:S(2)}, u32[]{:S(2)}) async-start(bf16[16,64,896]{2,1,0:T(8,128)(2,1)} %block.1), calls=%async_computation | async-start | bytes 3670016 | tf_op jit(solution)/shard_map/all_to_all | solution.py:363
  62.5 12.5 %collective-permute-start.16 = (bf16[64,768]{1,0:T(8,128)(2,1)}, bf16[64,768]{1,0:T(8,128)(2,1)S(1)}, u32[]{:S(2)}, u32[]{:S(2)}) collective-permute-start(bf16[64,768]{1,0:T(8,128)(2,1)} %get-tuple-element.49), channel_id=1, source_target_pairs={{0,32},{16,240},{32,64},{48,16},{64,96},{80,48},{96,128},{112,80},... | collective-permute-start | bytes 294920 | tf_op jit(solution)/shard_map/ppermute | solution.py:375
  65.8 10.6 %collective-permute-start.17 = (bf16[64,768]{1,0:T(8,128)(2,1)}, bf16[64,768]{1,0:T(8,128)(2,1)S(1)}, u32[]{:S(2)}, u32[]{:S(2)}) collective-permute-start(bf16[64,768]{1,0:T(8,128)(2,1)} %get-tuple-element.50), channel_id=1, source_target_pairs={{0,64},{16,208},{32,96},{48,240},{64,128},{80,16},{96,160},{112,48... | collective-permute-start | bytes 294920 | tf_op jit(solution)/shard_map/ppermute | solution.py:375
  68.8 11.3 %collective-permute-start.18 = (bf16[64,768]{1,0:T(8,128)(2,1)}, bf16[64,768]{1,0:T(8,128)(2,1)S(1)}, u32[]{:S(2)}, u32[]{:S(2)}) collective-permute-start(bf16[64,768]{1,0:T(8,128)(2,1)} %get-tuple-element.51), channel_id=1, source_target_pairs={{0,96},{16,176},{32,128},{48,208},{64,160},{80,240},{96,192},{112,... | collective-permute-start | bytes 294920 | tf_op jit(solution)/shard_map/ppermute | solution.py:375
  68.8 12.8 %collective-permute-start.19 = (bf16[64,768]{1,0:T(8,128)(2,1)}, bf16[64,768]{1,0:T(8,128)(2,1)S(1)}, u32[]{:S(2)}, u32[]{:S(2)}) collective-permute-start(bf16[64,768]{1,0:T(8,128)(2,1)} %get-tuple-element.52), channel_id=1, source_target_pairs={{0,128},{16,144},{32,160},{48,176},{64,192},{80,208},{96,224},{112... | collective-permute-start | bytes 294920 | tf_op jit(solution)/shard_map/ppermute | solution.py:375
  75.0 10.9 %collective-permute-start.20 = (bf16[64,768]{1,0:T(8,128)(2,1)}, bf16[64,768]{1,0:T(8,128)(2,1)S(1)}, u32[]{:S(2)}, u32[]{:S(2)}) collective-permute-start(bf16[64,768]{1,0:T(8,128)(2,1)} %get-tuple-element.53), channel_id=1, source_target_pairs={{0,160},{16,112},{32,192},{48,144},{64,224},{80,176},{96,0},{112,2... | collective-permute-start | bytes 294920 | tf_op jit(solution)/shard_map/ppermute | solution.py:375
  75.0 10.9 %copy-start.40 = (bf16[64,768]{1,0:T(8,128)(2,1)}, bf16[64,768]{1,0:T(8,128)(2,1)S(1)}, u32[]{:S(2)}) copy-start(bf16[64,768]{1,0:T(8,128)(2,1)S(1)} %collective-permute-done.16.refs_1_) | copy-start | bytes 294916
  75.0 10.9 %collective-permute-start.21 = (bf16[64,768]{1,0:T(8,128)(2,1)}, bf16[64,768]{1,0:T(8,128)(2,1)S(1)}, u32[]{:S(2)}, u32[]{:S(2)}) collective-permute-start(bf16[64,768]{1,0:T(8,128)(2,1)} %get-tuple-element.54), channel_id=1, source_target_pairs={{0,192},{16,80},{32,224},{48,112},{64,0},{80,144},{96,32},{112,176... | collective-permute-start | bytes 294920 | tf_op jit(solution)/shard_map/ppermute | solution.py:375
  76.4 9.4 %copy-start.41 = (bf16[64,768]{1,0:T(8,128)(2,1)}, bf16[64,768]{1,0:T(8,128)(2,1)S(1)}, u32[]{:S(2)}) copy-start(bf16[64,768]{1,0:T(8,128)(2,1)S(1)} %collective-permute-done.17.refs_2_) | copy-start | bytes 294916
  76.4 9.4 %collective-permute-start.22 = (bf16[64,768]{1,0:T(8,128)(2,1)}, bf16[64,768]{1,0:T(8,128)(2,1)S(1)}, u32[]{:S(2)}, u32[]{:S(2)}) collective-permute-start(bf16[64,768]{1,0:T(8,128)(2,1)} %get-tuple-element.55), channel_id=1, source_target_pairs={{0,224},{16,48},{32,0},{48,80},{64,32},{80,112},{96,64},{112,144},... | collective-permute-start | bytes 294920 | tf_op jit(solution)/shard_map/ppermute | solution.py:375
  80.1 5.8 %copy-start.42 = (bf16[64,768]{1,0:T(8,128)(2,1)}, bf16[64,768]{1,0:T(8,128)(2,1)S(1)}, u32[]{:S(2)}) copy-start(bf16[64,768]{1,0:T(8,128)(2,1)S(1)} %collective-permute-done.18.refs_3_) | copy-start | bytes 294916
  81.7 4.2 %copy-start.43 = (bf16[64,768]{1,0:T(8,128)(2,1)}, bf16[64,768]{1,0:T(8,128)(2,1)S(1)}, u32[]{:S(2)}) copy-start(bf16[64,768]{1,0:T(8,128)(2,1)S(1)} %collective-permute-done.19.refs_4_) | copy-start | bytes 294916
  88.7 24.0 %collective-permute-start.24 = (bf16[8,64,768]{2,1,0:T(8,128)(2,1)}, bf16[8,64,768]{2,1,0:T(8,128)(2,1)S(1)}, u32[]{:S(2)}, u32[]{:S(2)}) collective-permute-start(bf16[8,64,768]{2,1,0:T(8,128)(2,1)} %get-tuple-element.59.refs_16_), channel_id=1, source_target_pairs={{0,1},{1,0},{2,3},{3,2},{4,5},{5,4},{6,7},{7,6},{8,9},{9,8},{10,11... | collective-permute-start | bytes 2359304 | tf_op jit(solution)/shard_map/ppermute | solution.py:384
  91.6 0.7 collective-permute-start.23
  93.7 19.0 %copy-start.4 = (bf16[64,1536]{1,0:T(8,128)(2,1)S(1)}, bf16[64,1536]{1,0:T(8,128)(2,1)}, u32[]{:S(2)}) copy-start(bf16[64,1536]{1,0:T(8,128)(2,1)} %copy-done.3) | copy-start | bytes 589828
  93.7 19.0 %copy-start.6 = (bf16[64,1536]{1,0:T(8,128)(2,1)S(1)}, bf16[64,1536]{1,0:T(8,128)(2,1)}, u32[]{:S(2)}) copy-start(bf16[64,1536]{1,0:T(8,128)(2,1)} %copy-done.5) | copy-start | bytes 589828
  93.7 19.0 %copy-start.8 = (bf16[64,1536]{1,0:T(8,128)(2,1)S(1)}, bf16[64,1536]{1,0:T(8,128)(2,1)}, u32[]{:S(2)}) copy-start(bf16[64,1536]{1,0:T(8,128)(2,1)} %copy-done.7) | copy-start | bytes 589828
  93.7 19.1 %copy-start.10 = (bf16[64,1536]{1,0:T(8,128)(2,1)S(1)}, bf16[64,1536]{1,0:T(8,128)(2,1)}, u32[]{:S(2)}) copy-start(bf16[64,1536]{1,0:T(8,128)(2,1)} %copy-done.9) | copy-start | bytes 589828
  93.7 19.1 %copy-start.12 = (bf16[64,1536]{1,0:T(8,128)(2,1)S(1)}, bf16[64,1536]{1,0:T(8,128)(2,1)}, u32[]{:S(2)}) copy-start(bf16[64,1536]{1,0:T(8,128)(2,1)} %copy-done.11) | copy-start | bytes 589828
  93.7 19.1 %copy-start.14 = (bf16[64,1536]{1,0:T(8,128)(2,1)S(1)}, bf16[64,1536]{1,0:T(8,128)(2,1)}, u32[]{:S(2)}) copy-start(bf16[64,1536]{1,0:T(8,128)(2,1)} %copy-done.13) | copy-start | bytes 589828
  93.7 19.1 %copy-start.16 = (bf16[64,1536]{1,0:T(8,128)(2,1)S(1)}, bf16[64,1536]{1,0:T(8,128)(2,1)}, u32[]{:S(2)}) copy-start(bf16[64,1536]{1,0:T(8,128)(2,1)} %copy-done.15) | copy-start | bytes 589828
  93.7 19.1 %copy-start.18 = (bf16[64,1536]{1,0:T(8,128)(2,1)S(1)}, bf16[64,1536]{1,0:T(8,128)(2,1)}, u32[]{:S(2)}) copy-start(bf16[64,1536]{1,0:T(8,128)(2,1)} %copy-done.17) | copy-start | bytes 589828
  93.7 19.1 %copy-start.20 = (s32[3]{0:T(128)S(1)}, s32[3]{0:T(128)}, u32[]{:S(2)}) copy-start(s32[3]{0:T(128)} %pad_add_fusion.refs_0_.at_ref) | copy-start | bytes 40
  93.7 19.1 %copy-start.22 = (bf16[8,64,768]{2,1,0:T(8,128)(2,1)S(1)}, bf16[8,64,768]{2,1,0:T(8,128)(2,1)}, u32[]{:S(2)}) copy-start(bf16[8,64,768]{2,1,0:T(8,128)(2,1)} %get-tuple-element.59.refs_16_) | copy-start | bytes 2359300
  93.7 19.1 %copy-start.24 = (bf16[64,1536]{1,0:T(8,128)(2,1)S(1)}, bf16[64,1536]{1,0:T(8,128)(2,1)}, u32[]{:S(2)}) copy-start(bf16[64,1536]{1,0:T(8,128)(2,1)} %get-tuple-element.34.first_ref.refs_1_.refs_0_) | copy-start | bytes 589828
  93.7 19.1 %copy-start.26 = (bf16[64,1536]{1,0:T(8,128)(2,1)S(1)}, bf16[64,1536]{1,0:T(8,128)(2,1)}, u32[]{:S(2)}) copy-start(bf16[64,1536]{1,0:T(8,128)(2,1)} %get-tuple-element.35.second_ref.refs_2_.refs_1_) | copy-start | bytes 589828
  93.8 43.6 %all-to-all-start.1 = ((bf16[16,64,896]{2,1,0:T(8,128)(2,1)}), bf16[16,64,896]{2,1,0:T(8,128)(2,1)}, u32[]{:S(2)}, u32[]{:S(2)}) async-start(bf16[16,64,896]{2,1,0:T(8,128)(2,1)} %get-tuple-element.57), calls=%async_computation.1 | async-start | bytes 3670016 | tf_op jit(solution)/shard_map/all_to_all | solution.py:391
  112.8 0.9 copy-start.28
  121.9 1.0 copy-start.2
  122.9 3.1 %collective-permute-start.25 = (bf16[384,1536]{1,0:T(8,128)(2,1)}, bf16[384,1536]{1,0:T(8,128)(2,1)S(1)}, u32[]{:S(2)}, u32[]{:S(2)}) collective-permute-start(bf16[384,1536]{1,0:T(8,128)(2,1)} %get-tuple-element.61), channel_id=1, source_target_pairs={{0,16},{16,0},{32,48},{48,32},{64,80},{80,64},{96,112},{112,96},{1... | collective-permute-start | bytes 3538952 | tf_op jit(solution)/shard_map/ppermute | solution.py:403
  126.0 11.4 %copy-start.39 = (bf16[384,1536]{1,0:T(8,128)(2,1)}, bf16[384,1536]{1,0:T(8,128)(2,1)S(1)}, u32[]{:S(2)}) copy-start(bf16[384,1536]{1,0:T(8,128)(2,1)S(1)} %collective-permute-done.25.come_hbm) | copy-start | bytes 3538948
  (12 other events, 9.9 us)

commit v3 on v2

--- a/solution.py
+++ b/solution.py
@@ -371,7 +371,7 @@
         [pltpu.VMEM((HALF, D), jnp.bfloat16), pltpu.VMEM((NZ, HALF, CHIP), jnp.bfloat16), dma(NZ + 1)],
     )(place, inputs)
     come_in = {0: pieces[0]}
-    for k in (1, 7, 2, 6, 3, 5, 4):
+    for k in (4, 3, 5, 2, 6, 1, 7):
         come_in[k] = lax.ppermute(pieces[k], "dp", ring_perm(k))
     mine, here = call(
         stack_kernel,
@@ -382,7 +382,8 @@
         [dma(NZ)],
     )(*[come_in[k] for k in range(NZ)])
     theirs = lax.ppermute(mine, "tensor", [(n, n ^ 1) for n in range(NT)])
-    summed = call(sum_kernel, [VMEM] * 2, VMEM, shape((HALF, WIDE)), "sum", mib=16)(swapped, here)
+    early = gate([come_in[k] for k in (4, 3, 5)])
+    summed = call(sum_kernel, [VMEM] * 2, VMEM, shape((HALF, WIDE)), "sum", mib=16)(swapped, early)
     back = lax.ppermute(summed, ("dp", "tensor"), spread_perm(-1))
 
     copies, token = call(

time: 145 us -> 144 us (level); the launches traced: 143 us -> 143 us
  starting transfers between devices: 67.9 us -> 63.7 us
  waiting for transfers between devices: 29.8 us -> 33.8 us
    ppermute x7, waiting for transfers between devices: 6.72 us -> 9.68 us  [on_device(): come_in[k] = lax.ppermute(pieces[k], 'dp', ring_perm(k))]
    all_to_all x1, starting transfers between devices: 18.9 us -> 16.3 us  [on_device(): whole = lax.all_to_all(copies, 'tensor', 0, 0)]
    unnamed x96 -> x98, local copies, waits for them, and re-layouts: 11.9 us -> 11.9 us
where the time goes in v3:
time: 144 us; the launch traced here: 143 us
  starting transfers between devices  63.7 us (44%)
  waiting for transfers between devices  33.8 us (23%)
  Pallas kernels  31.6 us (22%)
  local copies, waits for them, and re-layouts  11.9 us (8%)
  between operations  1.5 us (1%)
    ppermute x14, starting transfers between devices, step(): lax.ppermute(chunks[n], 'dp', ring_perm(sign))  22.5 us
    all_to_all x1, starting transfers between devices, on_device(): whole = lax.all_to_all(copies, 'tensor', 0, 0)  16.3 us
    ppermute x7, starting transfers between devices, on_device(): come_in[k] = lax.ppermute(pieces[k], 'dp', ring_perm(k))  15.2 us
    all_to_all x1, waiting for transfers between devices, on_device(): whole = lax.all_to_all(copies, 'tensor', 0, 0)  12.6 us
    unnamed x98, local copies, waits for them, and re-layouts  11.9 us
    ppermute x7, waiting for transfers between devices, on_device(): come_in[k] = lax.ppermute(pieces[k], 'dp', ring_perm(k))  9.68 us
    ppermute x14, waiting for transfers between devices, step(): lax.ppermute(chunks[n], 'dp', ring_perm(sign))  8.52 us
    pallas_call x1, Pallas kernels, on_device(): call(block_kernel, [SMEM] + [HBM] * (NT + 2) + [VMEM] * 2, HBM, shape((NT...  7.53 us
  transfers between devices with their start and end apart: 28, of which 8 were waited for; matrix products, arithmetic and copies ran while one was open for 0% of the time, Pallas kernels for 13%

profile of v3, /device:TPU:32, one launch (start us, length us, event | category | flops | bytes accessed | tf_op | source)
XLA Modules:
  0.0 143.1 jit_solution(7686975627005887659)
XLA Ops:
  0.6 0.1 collective-permute-start.14
  0.7 2.4 %slope.1 = (bf16[64,1536]{1,0:T(8,128)(2,1)}, bf16[64,1536]{1,0:T(8,128)(2,1)}) custom-call(bf16[128,1536]{1,0:T(8,128)(2,1)} %pre_hbm.1, bf16[128,1536]{1,0:T(8,128)(2,1)} %act_hbm.1), custom_call_target="tpu_custom_call" | custom-call | bytes 1048576 | tf_op jit(solution)/shard_map/slope/pallas_call | solution.py:298
  3.1 2.0 %collective-permute-start = (bf16[64,1536]{1,0:T(8,128)(2,1)}, bf16[64,1536]{1,0:T(8,128)(2,1)S(1)}, u32[]{:S(2)}, u32[]{:S(2)}) collective-permute-start(bf16[64,1536]{1,0:T(8,128)(2,1)} %get-tuple-element.34.first_ref.refs_1_.refs_0_), channel_id=1, source_target_pairs={{0,32},{16,240},{32,64},{48,16},{64,96},{80,48},{96,128},{112,80},... | collective-permute-start | bytes 589832 | tf_op jit(solution)/shard_map/ppermute | solution.py:319
  5.1 0.1 collective-permute-start.1
  5.2 1.9 %collective-permute-start.2 = (bf16[64,1536]{1,0:T(8,128)(2,1)}, bf16[64,1536]{1,0:T(8,128)(2,1)S(1)}, u32[]{:S(2)}, u32[]{:S(2)}) collective-permute-start(bf16[64,1536]{1,0:T(8,128)(2,1)} %get-tuple-element.35.second_ref.refs_2_.refs_1_), channel_id=1, source_target_pairs={{0,32},{16,240},{32,64},{48,16},{64,96},{80,48},{96,128},{112,80},... | collective-permute-start | bytes 589832 | tf_op jit(solution)/shard_map/ppermute | solution.py:319
  7.1 2.1 %collective-permute-start.3 = (bf16[64,1536]{1,0:T(8,128)(2,1)}, bf16[64,1536]{1,0:T(8,128)(2,1)S(1)}, u32[]{:S(2)}, u32[]{:S(2)}) collective-permute-start(bf16[64,1536]{1,0:T(8,128)(2,1)} %get-tuple-element.35.second_ref.refs_2_.refs_1_), channel_id=1, source_target_pairs={{0,224},{16,48},{32,0},{48,80},{64,32},{80,112},{96,64},{112,144},... | collective-permute-start | bytes 589832 | tf_op jit(solution)/shard_map/ppermute | solution.py:319
  9.2 1.4 copy-done
  10.7 0.9 copy-done.24
  11.6 0.9 copy-done.26
  12.5 1.5 %amax.4.refs_2_ = f32[8,128]{1,0:T(8,128)S(1)} custom-call(f32[8,128]{1,0:T(8,128)S(1)} %broadcast_in_dim.3.before_ref, bf16[128,6144]{1,0:T(8,128)(2,1)S(1)} %copy-done, bf16[64,1536]{1,0:T(8,128)(2,1)S(1)} %copy-done.24, bf16[64,1536]{1,0:T(8,128)(2,1)S(1)} %copy-done.26), custom_call_target="tpu_custom_call" | custom-call | flops 603979776 | bytes 1048576 | tf_op jit(solution)/shard_map/amax/pallas_call | solution.py:323
  14.1 0.0 collective-permute-done.refs_0_
  14.1 0.0 collective-permute-done.1.refs_1_
  14.1 1.7 %collective-permute-start.4 = (bf16[64,1536]{1,0:T(8,128)(2,1)S(1)}, bf16[64,1536]{1,0:T(8,128)(2,1)S(1)}, u32[]{:S(2)}, u32[]{:S(2)}) collective-permute-start(bf16[64,1536]{1,0:T(8,128)(2,1)S(1)} %get-tuple-element.36.refs_3_.refs_2_), channel_id=1, source_target_pairs={{0,32},{16,240},{32,64},{48,16},{64,96},{80,48},{96,128},{112,80},... | collective-permute-start | bytes 589832 | tf_op jit(solution)/shard_map/ppermute | solution.py:319
  15.8 1.7 %collective-permute-start.5 = (bf16[64,1536]{1,0:T(8,128)(2,1)S(1)}, bf16[64,1536]{1,0:T(8,128)(2,1)S(1)}, u32[]{:S(2)}, u32[]{:S(2)}) collective-permute-start(bf16[64,1536]{1,0:T(8,128)(2,1)S(1)} %get-tuple-element.39.refs_15_.refs_14_), channel_id=1, source_target_pairs={{0,224},{16,48},{32,0},{48,80},{64,32},{80,112},{96,64},{112,144},... | collective-permute-start | bytes 589832 | tf_op jit(solution)/shard_map/ppermute | solution.py:319
  17.5 1.5 %amax.5.refs_2_ = f32[8,128]{1,0:T(8,128)S(1)} custom-call(f32[8,128]{1,0:T(8,128)S(1)} %get-tuple-element.37.before_ref, bf16[128,6144]{1,0:T(8,128)(2,1)S(1)} %copy-done.1, bf16[64,1536]{1,0:T(8,128)(2,1)S(1)} %copy-done.24, bf16[64,1536]{1,0:T(8,128)(2,1)S(1)} %copy-done.26), custom_call_target="tpu_custom_call" | custom-call | flops 603979776 | bytes 1048576 | tf_op jit(solution)/shard_map/amax/pallas_call | solution.py:323
  19.0 0.0 collective-permute-done.2.refs_0_
  19.1 1.3 collective-permute-start.6
  20.4 2.1 %collective-permute-start.7 = (bf16[64,1536]{1,0:T(8,128)(2,1)S(1)}, bf16[64,1536]{1,0:T(8,128)(2,1)S(1)}, u32[]{:S(2)}, u32[]{:S(2)}) collective-permute-start(bf16[64,1536]{1,0:T(8,128)(2,1)S(1)} %get-tuple-element.42.refs_16_.refs_15_), channel_id=1, source_target_pairs={{0,224},{16,48},{32,0},{48,80},{64,32},{80,112},{96,64},{112,144},... | collective-permute-start | bytes 589832 | tf_op jit(solution)/shard_map/ppermute | solution.py:319
  22.4 1.5 %amax.6.refs_2_ = f32[8,128]{1,0:T(8,128)S(1)} custom-call(f32[8,128]{1,0:T(8,128)S(1)} %get-tuple-element.40.before_ref, bf16[128,6144]{1,0:T(8,128)(2,1)S(1)} %copy-done.1, bf16[64,1536]{1,0:T(8,128)(2,1)S(1)} %copy-done.24, bf16[64,1536]{1,0:T(8,128)(2,1)S(1)} %copy-done.26), custom_call_target="tpu_custom_call" | custom-call | flops 603979776 | bytes 1048576 | tf_op jit(solution)/shard_map/amax/pallas_call | solution.py:323
  24.0 3.1 %collective-permute-start.8 = (bf16[64,1536]{1,0:T(8,128)(2,1)S(1)}, bf16[64,1536]{1,0:T(8,128)(2,1)S(1)}, u32[]{:S(2)}, u32[]{:S(2)}) collective-permute-start(bf16[64,1536]{1,0:T(8,128)(2,1)S(1)} %get-tuple-element.41.refs_5_.refs_4_), channel_id=1, source_target_pairs={{0,32},{16,240},{32,64},{48,16},{64,96},{80,48},{96,128},{112,80},... | collective-permute-start | bytes 589832 | tf_op jit(solution)/shard_map/ppermute | solution.py:319
  27.2 1.5 %amax.7.refs_2_ = f32[8,128]{1,0:T(8,128)S(1)} custom-call(f32[8,128]{1,0:T(8,128)S(1)} %get-tuple-element.43.before_ref, bf16[128,6144]{1,0:T(8,128)(2,1)S(1)} %copy-done.1, bf16[64,1536]{1,0:T(8,128)(2,1)S(1)} %copy-done.24, bf16[64,1536]{1,0:T(8,128)(2,1)S(1)} %copy-done.26), custom_call_target="tpu_custom_call" | custom-call | flops 603979776 | bytes 1048576 | tf_op jit(solution)/shard_map/amax/pallas_call | solution.py:323
  28.8 0.0 copy-start.21
  28.8 1.9 %collective-permute-start.11 = (bf16[64,1536]{1,0:T(8,128)(2,1)S(1)}, bf16[64,1536]{1,0:T(8,128)(2,1)S(1)}, u32[]{:S(2)}, u32[]{:S(2)}) collective-permute-start(bf16[64,1536]{1,0:T(8,128)(2,1)S(1)} %get-tuple-element.45.refs_14_.refs_13_), channel_id=1, source_target_pairs={{0,224},{16,48},{32,0},{48,80},{64,32},{80,112},{96,64},{112,144},... | collective-permute-start | bytes 589832 | tf_op jit(solution)/shard_map/ppermute | solution.py:319
  30.7 1.6 %collective-permute-start.9 = (bf16[64,1536]{1,0:T(8,128)(2,1)S(1)}, bf16[64,1536]{1,0:T(8,128)(2,1)S(1)}, u32[]{:S(2)}, u32[]{:S(2)}) collective-permute-start(bf16[64,1536]{1,0:T(8,128)(2,1)S(1)} %get-tuple-element.44.refs_6_.refs_5_), channel_id=1, source_target_pairs={{0,32},{16,240},{32,64},{48,16},{64,96},{80,48},{96,128},{112,80},... | collective-permute-start | bytes 589832 | tf_op jit(solution)/shard_map/ppermute | solution.py:319
  32.3 1.4 collective-permute-start.13
  33.7 1.7 %collective-permute-start.10 = (bf16[64,1536]{1,0:T(8,128)(2,1)S(1)}, bf16[64,1536]{1,0:T(8,128)(2,1)S(1)}, u32[]{:S(2)}, u32[]{:S(2)}) collective-permute-start(bf16[64,1536]{1,0:T(8,128)(2,1)S(1)} %collective-permute-done.8.refs_7_.refs_6_), channel_id=1, source_target_pairs={{0,32},{16,240},{32,64},{48,16},{64,96},{80,48},{96,128},{112,80},... | collective-permute-start | bytes 589832 | tf_op jit(solution)/shard_map/ppermute | solution.py:319
  35.4 2.4 %collective-permute-done.11.refs_12_.refs_11_ = bf16[64,1536]{1,0:T(8,128)(2,1)S(1)} collective-permute-done((bf16[64,1536]{1,0:T(8,128)(2,1)S(1)}, bf16[64,1536]{1,0:T(8,128)(2,1)S(1)}, u32[]{:S(2)}, u32[]{:S(2)}) %collective-permute-start.11) | collective-permute-done | bytes 196640 | tf_op jit(solution)/shard_map/ppermute | solution.py:319
  37.8 0.6 pad_add_fusion.refs_0_.at_ref
  38.4 3.6 %collective-permute-done.13.refs_11_.refs_10_ = bf16[64,1536]{1,0:T(8,128)(2,1)S(1)} collective-permute-done((bf16[64,1536]{1,0:T(8,128)(2,1)S(1)}, bf16[64,1536]{1,0:T(8,128)(2,1)S(1)}, u32[]{:S(2)}, u32[]{:S(2)}) %collective-permute-start.13) | collective-permute-done | bytes 196640 | tf_op jit(solution)/shard_map/ppermute | solution.py:319
  42.0 2.5 %collective-permute-done.12.refs_10_.refs_9_ = bf16[64,1536]{1,0:T(8,128)(2,1)S(1)} collective-permute-done((bf16[64,1536]{1,0:T(8,128)(2,1)S(1)}, bf16[64,1536]{1,0:T(8,128)(2,1)S(1)}, u32[]{:S(2)}, u32[]{:S(2)}) %collective-permute-start.12) | collective-permute-done | bytes 196640 | tf_op jit(solution)/shard_map/ppermute | solution.py:319
  44.6 0.6 copy-done.38
  45.2 7.5 %block.1 = bf16[16,64,896]{2,1,0:T(8,128)(2,1)} custom-call(s32[3]{0:T(128)} %pad_add_fusion.refs_0_.at_ref, bf16[64,1536]{1,0:T(8,128)(2,1)} %get-tuple-element.34.first_ref.refs_1_.refs_0_, bf16[64,1536]{1,0:T(8,128)(2,1)} %get-tuple-element.35.second_ref.refs_2_.refs_1_, bf16[64,1536]{1,0:T(8,128)(2,1)} %copy-done.15, bf16[64,1536]{1,0:T(8,128)(2,1)} %copy-done.3, ...), custom_call_target="tpu_custom_call" | custom-call | flops 2415919104 | bytes 7340032 | tf_op jit(solution)/shard_map/block/pallas_call | solution.py:347
  52.7 7.0 %all-to-all-start = ((bf16[16,64,896]{2,1,0:T(8,128)(2,1)}), bf16[16,64,896]{2,1,0:T(8,128)(2,1)S(1)}, u32[]{:S(2)}, u32[]{:S(2)}) async-start(bf16[16,64,896]{2,1,0:T(8,128)(2,1)} %block.1), calls=%async_computation | async-start | bytes 3670016 | tf_op jit(solution)/shard_map/all_to_all | solution.py:363
  59.8 2.7 %pick.1 = (bf16[64,768]{1,0:T(8,128)(2,1)}, bf16[64,768]{1,0:T(8,128)(2,1)}, bf16[64,768]{1,0:T(8,128)(2,1)}, bf16[64,768]{1,0:T(8,128)(2,1)}, bf16[64,768]{1,0:...) custom-call(s32[3]{0:T(128)} %pad_add_fusion.refs_0_.at_ref, ...), custom_call_target="tpu_custom_call" | custom-call | bytes 1048576 | tf_op jit(solution)/shard_map/pick/pallas_call | solution.py:365
  62.5 3.4 %collective-permute-start.16 = (bf16[64,768]{1,0:T(8,128)(2,1)}, bf16[64,768]{1,0:T(8,128)(2,1)S(1)}, u32[]{:S(2)}, u32[]{:S(2)}) collective-permute-start(bf16[64,768]{1,0:T(8,128)(2,1)} %get-tuple-element.48), channel_id=1, source_target_pairs={{0,128},{16,144},{32,160},{48,176},{64,192},{80,208},{96,224},{112... | collective-permute-start | bytes 294920 | tf_op jit(solution)/shard_map/ppermute | solution.py:375
  65.9 2.5 %collective-permute-start.17 = (bf16[64,768]{1,0:T(8,128)(2,1)}, bf16[64,768]{1,0:T(8,128)(2,1)S(1)}, u32[]{:S(2)}, u32[]{:S(2)}) collective-permute-start(bf16[64,768]{1,0:T(8,128)(2,1)} %get-tuple-element.49), channel_id=1, source_target_pairs={{0,96},{16,176},{32,128},{48,208},{64,160},{80,240},{96,192},{112,... | collective-permute-start | bytes 294920 | tf_op jit(solution)/shard_map/ppermute | solution.py:375
  68.4 2.6 %collective-permute-start.18 = (bf16[64,768]{1,0:T(8,128)(2,1)}, bf16[64,768]{1,0:T(8,128)(2,1)S(1)}, u32[]{:S(2)}, u32[]{:S(2)}) collective-permute-start(bf16[64,768]{1,0:T(8,128)(2,1)} %get-tuple-element.50), channel_id=1, source_target_pairs={{0,160},{16,112},{32,192},{48,144},{64,224},{80,176},{96,0},{112,2... | collective-permute-start | bytes 294920 | tf_op jit(solution)/shard_map/ppermute | solution.py:375
  71.0 2.6 %collective-permute-start.20 = (bf16[64,768]{1,0:T(8,128)(2,1)}, bf16[64,768]{1,0:T(8,128)(2,1)S(1)}, u32[]{:S(2)}, u32[]{:S(2)}) collective-permute-start(bf16[64,768]{1,0:T(8,128)(2,1)} %get-tuple-element.52), channel_id=1, source_target_pairs={{0,32},{16,240},{32,64},{48,16},{64,96},{80,48},{96,128},{112,80},... | collective-permute-start | bytes 294920 | tf_op jit(solution)/shard_map/ppermute | solution.py:375
  73.5 1.5 %collective-permute-start.21 = (bf16[64,768]{1,0:T(8,128)(2,1)}, bf16[64,768]{1,0:T(8,128)(2,1)S(1)}, u32[]{:S(2)}, u32[]{:S(2)}) collective-permute-start(bf16[64,768]{1,0:T(8,128)(2,1)} %get-tuple-element.53), channel_id=1, source_target_pairs={{0,64},{16,208},{32,96},{48,240},{64,128},{80,16},{96,160},{112,48... | collective-permute-start | bytes 294920 | tf_op jit(solution)/shard_map/ppermute | solution.py:375
  75.0 2.7 %collective-permute-start.22 = (bf16[64,768]{1,0:T(8,128)(2,1)}, bf16[64,768]{1,0:T(8,128)(2,1)S(1)}, u32[]{:S(2)}, u32[]{:S(2)}) collective-permute-start(bf16[64,768]{1,0:T(8,128)(2,1)} %get-tuple-element.54), channel_id=1, source_target_pairs={{0,192},{16,80},{32,224},{48,112},{64,0},{80,144},{96,32},{112,176... | collective-permute-start | bytes 294920 | tf_op jit(solution)/shard_map/ppermute | solution.py:375
  77.7 4.9 %collective-permute-done.17.refs_1_.refs_3_ = bf16[64,768]{1,0:T(8,128)(2,1)S(1)} collective-permute-done((bf16[64,768]{1,0:T(8,128)(2,1)}, bf16[64,768]{1,0:T(8,128)(2,1)S(1)}, u32[]{:S(2)}, u32[]{:S(2)}) %collective-permute-start.17) | collective-permute-done | bytes 98336 | tf_op jit(solution)/shard_map/ppermute | solution.py:375
  82.6 4.1 %collective-permute-done.21.refs_2_ = bf16[64,768]{1,0:T(8,128)(2,1)S(1)} collective-permute-done((bf16[64,768]{1,0:T(8,128)(2,1)}, bf16[64,768]{1,0:T(8,128)(2,1)S(1)}, u32[]{:S(2)}, u32[]{:S(2)}) %collective-permute-start.21) | collective-permute-done | bytes 98336 | tf_op jit(solution)/shard_map/ppermute | solution.py:375
  86.7 0.7 collective-permute-done.23.refs_7_
  87.4 0.6 copy-done.47
  88.0 2.2 %stack.17 = (bf16[8,64,768]{2,1,0:T(8,128)(2,1)}, f32[8,128]{1,0:T(8,128)}) custom-call(bf16[64,768]{1,0:T(8,128)(2,1)} %get-tuple-element.51.refs_0_, bf16[64,768]{1,0:T(8,128)(2,1)} %copy-done.44, bf16[64,768]{1,0:T(8,128)(2,1)} %copy-done.45, bf16[64,768]{1,0:T(8,128)(2,1)} %copy-done.42, bf16[64,768]{1,0:T(8,128)(2,1)} %copy-done.41, ...), custom_call_target="tpu_custom_call" | custom-call | bytes 1048576 | tf_op jit(solution)/shard_map/stack/pallas_call | solution.py:376
  90.2 1.9 %collective-permute-start.24 = (bf16[8,64,768]{2,1,0:T(8,128)(2,1)}, bf16[8,64,768]{2,1,0:T(8,128)(2,1)S(1)}, u32[]{:S(2)}, u32[]{:S(2)}) collective-permute-start(bf16[8,64,768]{2,1,0:T(8,128)(2,1)} %get-tuple-element.59.refs_16_), channel_id=1, source_target_pairs={{0,1},{1,0},{2,3},{3,2},{4,5},{5,4},{6,7},{7,6},{8,9},{9,8},{10,11... | collective-permute-start | bytes 2359304 | tf_op jit(solution)/shard_map/ppermute | solution.py:384
  92.1 0.6 gate.1._
  92.7 0.7 copy-done.19
  93.4 0.2 sum.1
  93.6 0.7 collective-permute-start.19
  94.3 1.4 spread.1
  95.7 0.0 copy-start.23
  95.8 16.3 %all-to-all-start.1 = ((bf16[16,64,896]{2,1,0:T(8,128)(2,1)}), bf16[16,64,896]{2,1,0:T(8,128)(2,1)}, u32[]{:S(2)}, u32[]{:S(2)}) async-start(bf16[16,64,896]{2,1,0:T(8,128)(2,1)} %get-tuple-element.57), calls=%async_computation.1 | async-start | bytes 3670016 | tf_op jit(solution)/shard_map/all_to_all | solution.py:392
  112.2 0.9 copy-done.29
  113.1 0.9 copy-done.31
  114.1 0.9 copy-done.33
  115.0 0.9 copy-done.35
  115.9 0.9 copy-done.37
  116.8 0.9 copy-done.39
  117.8 3.5 %outer.1 = (bf16[384,1536]{1,0:T(8,128)(2,1)S(1)}, bf16[384,1536]{1,0:T(8,128)(2,1)}) custom-call(s32[3]{0:T(128)S(1)} %copy-done.20, f32[8,128]{1,0:T(8,128)S(1)} %get-tuple-element.58._, bf16[64,1536]{1,0:T(8,128)(2,1)S(1)} %copy-done.25, bf16[64,1536]{1,0:T(8,128)(2,1)S(1)} %copy-done.27, bf16[64,1536]{1,0:T(8,128)(2,1)S(1)} %copy-done.16, ...), custom_call_target="tpu_custom_call" | custom-call | flops 2415919104 | bytes 9437184 | tf_op jit(solution)/shard_map/outer/pallas_call | solution.py:393
  121.3 1.0 copy-done.2
  122.3 3.1 %collective-permute-done.25.come_hbm = bf16[384,1536]{1,0:T(8,128)(2,1)S(1)} collective-permute-done((bf16[384,1536]{1,0:T(8,128)(2,1)}, bf16[384,1536]{1,0:T(8,128)(2,1)S(1)}, u32[]{:S(2)}, u32[]{:S(2)}) %collective-permute-start.25) | collective-permute-done | bytes 1179680 | tf_op jit(solution)/shard_map/ppermute | solution.py:404
  125.4 12.6 %all-to-all-done.1.whole_hbm = bf16[16,64,896]{2,1,0:T(8,128)(2,1)} async-done(((bf16[16,64,896]{2,1,0:T(8,128)(2,1)}), bf16[16,64,896]{2,1,0:T(8,128)(2,1)}, u32[]{:S(2)}, u32[]{:S(2)}) %all-to-all-start.1) | async-done | bytes 1835040 | tf_op jit(solution)/shard_map/all_to_all | solution.py:392
  137.9 5.0 %final.1 = (bf16[128,6144]{1,0:T(8,128)(2,1)}, f32[384,1536]{1,0:T(8,128)}, f32[1,1]{1,0:T(1,128)}) custom-call(s32[3]{0:T(128)} %pad_add_fusion.refs_0_.at_ref, bf16[16,64,896]{2,1,0:T(8,128)(2,1)} %all-to-all-done.1.whole_hbm, bf16[384,1536]{1,0:T(8,128)(2,1)} %copy-done.2, bf16[384,1536]{1,0:T(8,128)(2,1)} %copy-done.40), custom_call_target="tpu_custom_call" | custom-call | bytes 1048576 | tf_op jit(solution)/shard_map/final/pallas_call | solution.py:405
  (109 shorter events, 0.2 us)
Async XLA Ops:
  0.6 43.8 %collective-permute-start.14 = (bf16[384,1536]{1,0:T(8,128)(2,1)}, bf16[384,1536]{1,0:T(8,128)(2,1)}, u32[]{:S(2)}, u32[]{:S(2)}) collective-permute-start(bf16[384,1536]{1,0:T(8,128)(2,1)} %refs_17_.1), channel_id=1, source_target_pairs={{0,16},{16,0},{32,48},{48,32},{64,80},{80,64},{96,112},{112,96},{1... | collective-permute-start | bytes 3538952 | tf_op jit(solution)/shard_map/ppermute | solution.py:306
  3.1 10.9 %collective-permute-start = (bf16[64,1536]{1,0:T(8,128)(2,1)}, bf16[64,1536]{1,0:T(8,128)(2,1)S(1)}, u32[]{:S(2)}, u32[]{:S(2)}) collective-permute-start(bf16[64,1536]{1,0:T(8,128)(2,1)} %get-tuple-element.34.first_ref.refs_1_.refs_0_), channel_id=1, source_target_pairs={{0,32},{16,240},{32,64},{48,16},{64,96},{80,48},{96,128},{112,80},... | collective-permute-start | bytes 589832 | tf_op jit(solution)/shard_map/ppermute | solution.py:319
  5.1 9.0 %collective-permute-start.1 = (bf16[64,1536]{1,0:T(8,128)(2,1)}, bf16[64,1536]{1,0:T(8,128)(2,1)S(1)}, u32[]{:S(2)}, u32[]{:S(2)}) collective-permute-start(bf16[64,1536]{1,0:T(8,128)(2,1)} %get-tuple-element.34.first_ref.refs_1_.refs_0_), channel_id=1, source_target_pairs={{0,224},{16,48},{32,0},{48,80},{64,32},{80,112},{96,64},{112,144},... | collective-permute-start | bytes 589832 | tf_op jit(solution)/shard_map/ppermute | solution.py:319
  5.2 13.8 %collective-permute-start.2 = (bf16[64,1536]{1,0:T(8,128)(2,1)}, bf16[64,1536]{1,0:T(8,128)(2,1)S(1)}, u32[]{:S(2)}, u32[]{:S(2)}) collective-permute-start(bf16[64,1536]{1,0:T(8,128)(2,1)} %get-tuple-element.35.second_ref.refs_2_.refs_1_), channel_id=1, source_target_pairs={{0,32},{16,240},{32,64},{48,16},{64,96},{80,48},{96,128},{112,80},... | collective-permute-start | bytes 589832 | tf_op jit(solution)/shard_map/ppermute | solution.py:319
  7.1 11.9 %collective-permute-start.3 = (bf16[64,1536]{1,0:T(8,128)(2,1)}, bf16[64,1536]{1,0:T(8,128)(2,1)S(1)}, u32[]{:S(2)}, u32[]{:S(2)}) collective-permute-start(bf16[64,1536]{1,0:T(8,128)(2,1)} %get-tuple-element.35.second_ref.refs_2_.refs_1_), channel_id=1, source_target_pairs={{0,224},{16,48},{32,0},{48,80},{64,32},{80,112},{96,64},{112,144},... | collective-permute-start | bytes 589832 | tf_op jit(solution)/shard_map/ppermute | solution.py:319
  9.2 1.4 copy-start
  12.5 5.0 %copy-start.1 = (bf16[128,6144]{1,0:T(8,128)(2,1)S(1)}, bf16[128,6144]{1,0:T(8,128)(2,1)}, u32[]{:S(2)}) copy-start(bf16[128,6144]{1,0:T(8,128)(2,1)} %in_hbm.1) | copy-start | bytes 4718596
  14.1 9.9 %copy-start.15 = (bf16[64,1536]{1,0:T(8,128)(2,1)}, bf16[64,1536]{1,0:T(8,128)(2,1)S(1)}, u32[]{:S(2)}) copy-start(bf16[64,1536]{1,0:T(8,128)(2,1)S(1)} %get-tuple-element.36.refs_3_.refs_2_) | copy-start | bytes 589828
  14.1 9.9 %copy-start.17 = (bf16[64,1536]{1,0:T(8,128)(2,1)}, bf16[64,1536]{1,0:T(8,128)(2,1)S(1)}, u32[]{:S(2)}) copy-start(bf16[64,1536]{1,0:T(8,128)(2,1)S(1)} %get-tuple-element.39.refs_15_.refs_14_) | copy-start | bytes 589828
  14.1 9.9 %collective-permute-start.4 = (bf16[64,1536]{1,0:T(8,128)(2,1)S(1)}, bf16[64,1536]{1,0:T(8,128)(2,1)S(1)}, u32[]{:S(2)}, u32[]{:S(2)}) collective-permute-start(bf16[64,1536]{1,0:T(8,128)(2,1)S(1)} %get-tuple-element.36.refs_3_.refs_2_), channel_id=1, source_target_pairs={{0,32},{16,240},{32,64},{48,16},{64,96},{80,48},{96,128},{112,80},... | collective-permute-start | bytes 589832 | tf_op jit(solution)/shard_map/ppermute | solution.py:319
  15.8 8.2 %collective-permute-start.5 = (bf16[64,1536]{1,0:T(8,128)(2,1)S(1)}, bf16[64,1536]{1,0:T(8,128)(2,1)S(1)}, u32[]{:S(2)}, u32[]{:S(2)}) collective-permute-start(bf16[64,1536]{1,0:T(8,128)(2,1)S(1)} %get-tuple-element.39.refs_15_.refs_14_), channel_id=1, source_target_pairs={{0,224},{16,48},{32,0},{48,80},{64,32},{80,112},{96,64},{112,144},... | collective-permute-start | bytes 589832 | tf_op jit(solution)/shard_map/ppermute | solution.py:319
  19.1 9.6 %copy-start.3 = (bf16[64,1536]{1,0:T(8,128)(2,1)}, bf16[64,1536]{1,0:T(8,128)(2,1)S(1)}, u32[]{:S(2)}) copy-start(bf16[64,1536]{1,0:T(8,128)(2,1)S(1)} %get-tuple-element.38.refs_4_.refs_3_) | copy-start | bytes 589828
  19.1 9.6 %copy-start.7 = (bf16[64,1536]{1,0:T(8,128)(2,1)}, bf16[64,1536]{1,0:T(8,128)(2,1)S(1)}, u32[]{:S(2)}) copy-start(bf16[64,1536]{1,0:T(8,128)(2,1)S(1)} %get-tuple-element.42.refs_16_.refs_15_) | copy-start | bytes 589828
  19.1 9.6 %collective-permute-start.6 = (bf16[64,1536]{1,0:T(8,128)(2,1)S(1)}, bf16[64,1536]{1,0:T(8,128)(2,1)S(1)}, u32[]{:S(2)}, u32[]{:S(2)}) collective-permute-start(bf16[64,1536]{1,0:T(8,128)(2,1)S(1)} %get-tuple-element.38.refs_4_.refs_3_), channel_id=1, source_target_pairs={{0,32},{16,240},{32,64},{48,16},{64,96},{80,48},{96,128},{112,80},... | collective-permute-start | bytes 589832 | tf_op jit(solution)/shard_map/ppermute | solution.py:319
  20.4 8.4 %collective-permute-start.7 = (bf16[64,1536]{1,0:T(8,128)(2,1)S(1)}, bf16[64,1536]{1,0:T(8,128)(2,1)S(1)}, u32[]{:S(2)}, u32[]{:S(2)}) collective-permute-start(bf16[64,1536]{1,0:T(8,128)(2,1)S(1)} %get-tuple-element.42.refs_16_.refs_15_), channel_id=1, source_target_pairs={{0,224},{16,48},{32,0},{48,80},{64,32},{80,112},{96,64},{112,144},... | collective-permute-start | bytes 589832 | tf_op jit(solution)/shard_map/ppermute | solution.py:319
  24.0 20.5 %copy-start.5 = (bf16[64,1536]{1,0:T(8,128)(2,1)}, bf16[64,1536]{1,0:T(8,128)(2,1)S(1)}, u32[]{:S(2)}) copy-start(bf16[64,1536]{1,0:T(8,128)(2,1)S(1)} %get-tuple-element.41.refs_5_.refs_4_) | copy-start | bytes 589828
  24.0 20.5 %copy-start.9 = (bf16[64,1536]{1,0:T(8,128)(2,1)}, bf16[64,1536]{1,0:T(8,128)(2,1)S(1)}, u32[]{:S(2)}) copy-start(bf16[64,1536]{1,0:T(8,128)(2,1)S(1)} %get-tuple-element.46.refs_13_.refs_12_) | copy-start | bytes 589828
  24.0 9.7 %collective-permute-start.8 = (bf16[64,1536]{1,0:T(8,128)(2,1)S(1)}, bf16[64,1536]{1,0:T(8,128)(2,1)S(1)}, u32[]{:S(2)}, u32[]{:S(2)}) collective-permute-start(bf16[64,1536]{1,0:T(8,128)(2,1)S(1)} %get-tuple-element.41.refs_5_.refs_4_), channel_id=1, source_target_pairs={{0,32},{16,240},{32,64},{48,16},{64,96},{80,48},{96,128},{112,80},... | collective-permute-start | bytes 589832 | tf_op jit(solution)/shard_map/ppermute | solution.py:319
  28.7 15.7 %copy-start.11 = (bf16[64,1536]{1,0:T(8,128)(2,1)}, bf16[64,1536]{1,0:T(8,128)(2,1)S(1)}, u32[]{:S(2)}) copy-start(bf16[64,1536]{1,0:T(8,128)(2,1)S(1)} %get-tuple-element.44.refs_6_.refs_5_) | copy-start | bytes 589828
  28.8 15.7 %copy-start.13 = (bf16[64,1536]{1,0:T(8,128)(2,1)}, bf16[64,1536]{1,0:T(8,128)(2,1)S(1)}, u32[]{:S(2)}) copy-start(bf16[64,1536]{1,0:T(8,128)(2,1)S(1)} %get-tuple-element.45.refs_14_.refs_13_) | copy-start | bytes 589828
  28.8 15.7 %copy-start.21 = (f32[8,128]{1,0:T(8,128)}, f32[8,128]{1,0:T(8,128)S(1)}, u32[]{:S(2)}) copy-start(f32[8,128]{1,0:T(8,128)S(1)} %get-tuple-element.47.refs_19_) | copy-start | bytes 12292
  28.8 9.0 %collective-permute-start.11 = (bf16[64,1536]{1,0:T(8,128)(2,1)S(1)}, bf16[64,1536]{1,0:T(8,128)(2,1)S(1)}, u32[]{:S(2)}, u32[]{:S(2)}) collective-permute-start(bf16[64,1536]{1,0:T(8,128)(2,1)S(1)} %get-tuple-element.45.refs_14_.refs_13_), channel_id=1, source_target_pairs={{0,224},{16,48},{32,0},{48,80},{64,32},{80,112},{96,64},{112,144},... | collective-permute-start | bytes 589832 | tf_op jit(solution)/shard_map/ppermute | solution.py:319
  30.7 1.6 %collective-permute-start.15 = (f32[8,128]{1,0:T(8,128)S(1)}, f32[8,128]{1,0:T(8,128)S(1)}, u32[]{:S(2)}, u32[]{:S(2)}) collective-permute-start(f32[8,128]{1,0:T(8,128)S(1)} %get-tuple-element.47.refs_19_), channel_id=1, source_target_pairs={{0,16},{16,0},{32,48},{48,32},{64,80},{80,64},{96,112},{112,96},{1... | collective-permute-start | bytes 12296 | tf_op jit(solution)/shard_map/ppermute | solution.py:343
  30.7 7.6 %collective-permute-start.9 = (bf16[64,1536]{1,0:T(8,128)(2,1)S(1)}, bf16[64,1536]{1,0:T(8,128)(2,1)S(1)}, u32[]{:S(2)}, u32[]{:S(2)}) collective-permute-start(bf16[64,1536]{1,0:T(8,128)(2,1)S(1)} %get-tuple-element.44.refs_6_.refs_5_), channel_id=1, source_target_pairs={{0,32},{16,240},{32,64},{48,16},{64,96},{80,48},{96,128},{112,80},... | collective-permute-start | bytes 589832 | tf_op jit(solution)/shard_map/ppermute | solution.py:319
  32.3 12.2 %copy-start.48 = (f32[8,128]{1,0:T(8,128)}, f32[8,128]{1,0:T(8,128)S(1)}, u32[]{:S(2)}) copy-start(f32[8,128]{1,0:T(8,128)S(1)} %collective-permute-done.15.refs_20_) | copy-start | bytes 12292
  32.3 9.6 %collective-permute-start.13 = (bf16[64,1536]{1,0:T(8,128)(2,1)S(1)}, bf16[64,1536]{1,0:T(8,128)(2,1)S(1)}, u32[]{:S(2)}, u32[]{:S(2)}) collective-permute-start(bf16[64,1536]{1,0:T(8,128)(2,1)S(1)} %get-tuple-element.46.refs_13_.refs_12_), channel_id=1, source_target_pairs={{0,224},{16,48},{32,0},{48,80},{64,32},{80,112},{96,64},{112,144},... | collective-permute-start | bytes 589832 | tf_op jit(solution)/shard_map/ppermute | solution.py:319
  33.7 10.8 %copy-start.28 = (bf16[64,1536]{1,0:T(8,128)(2,1)}, bf16[64,1536]{1,0:T(8,128)(2,1)S(1)}, u32[]{:S(2)}) copy-start(bf16[64,1536]{1,0:T(8,128)(2,1)S(1)} %collective-permute-done.8.refs_7_.refs_6_) | copy-start | bytes 589828
  33.7 8.3 %collective-permute-start.10 = (bf16[64,1536]{1,0:T(8,128)(2,1)S(1)}, bf16[64,1536]{1,0:T(8,128)(2,1)S(1)}, u32[]{:S(2)}, u32[]{:S(2)}) collective-permute-start(bf16[64,1536]{1,0:T(8,128)(2,1)S(1)} %collective-permute-done.8.refs_7_.refs_6_), channel_id=1, source_target_pairs={{0,32},{16,240},{32,64},{48,16},{64,96},{80,48},{96,128},{112,80},... | collective-permute-start | bytes 589832 | tf_op jit(solution)/shard_map/ppermute | solution.py:319
  37.8 6.8 %copy-start.30 = (bf16[64,1536]{1,0:T(8,128)(2,1)}, bf16[64,1536]{1,0:T(8,128)(2,1)S(1)}, u32[]{:S(2)}) copy-start(bf16[64,1536]{1,0:T(8,128)(2,1)S(1)} %collective-permute-done.11.refs_12_.refs_11_) | copy-start | bytes 589828
  37.8 6.7 %collective-permute-start.12 = (bf16[64,1536]{1,0:T(8,128)(2,1)S(1)}, bf16[64,1536]{1,0:T(8,128)(2,1)S(1)}, u32[]{:S(2)}, u32[]{:S(2)}) collective-permute-start(bf16[64,1536]{1,0:T(8,128)(2,1)S(1)} %collective-permute-done.11.refs_12_.refs_11_), channel_id=1, source_target_pairs={{0,224},{16,48},{32,0},{48,80},{64,32},{80,112},{96,64},{112,144},... | collective-permute-start | bytes 589832 | tf_op jit(solution)/shard_map/ppermute | solution.py:319
  38.4 6.2 %copy-start.32 = (bf16[64,1536]{1,0:T(8,128)(2,1)}, bf16[64,1536]{1,0:T(8,128)(2,1)S(1)}, u32[]{:S(2)}) copy-start(bf16[64,1536]{1,0:T(8,128)(2,1)S(1)} %collective-permute-done.9.refs_8_.refs_7_) | copy-start | bytes 589828
  42.0 2.6 %copy-start.34 = (bf16[64,1536]{1,0:T(8,128)(2,1)}, bf16[64,1536]{1,0:T(8,128)(2,1)S(1)}, u32[]{:S(2)}) copy-start(bf16[64,1536]{1,0:T(8,128)(2,1)S(1)} %collective-permute-done.13.refs_11_.refs_10_) | copy-start | bytes 589828
  42.0 2.6 %copy-start.36 = (bf16[64,1536]{1,0:T(8,128)(2,1)}, bf16[64,1536]{1,0:T(8,128)(2,1)S(1)}, u32[]{:S(2)}) copy-start(bf16[64,1536]{1,0:T(8,128)(2,1)S(1)} %collective-permute-done.10.refs_9_.refs_8_) | copy-start | bytes 589828
  52.7 40.0 %all-to-all-start = ((bf16[16,64,896]{2,1,0:T(8,128)(2,1)}), bf16[16,64,896]{2,1,0:T(8,128)(2,1)S(1)}, u32[]{:S(2)}, u32[]{:S(2)}) async-start(bf16[16,64,896]{2,1,0:T(8,128)(2,1)} %block.1), calls=%async_computation | async-start | bytes 3670016 | tf_op jit(solution)/shard_map/all_to_all | solution.py:363
  62.5 12.5 %collective-permute-start.16 = (bf16[64,768]{1,0:T(8,128)(2,1)}, bf16[64,768]{1,0:T(8,128)(2,1)S(1)}, u32[]{:S(2)}, u32[]{:S(2)}) collective-permute-start(bf16[64,768]{1,0:T(8,128)(2,1)} %get-tuple-element.48), channel_id=1, source_target_pairs={{0,128},{16,144},{32,160},{48,176},{64,192},{80,208},{96,224},{112... | collective-permute-start | bytes 294920 | tf_op jit(solution)/shard_map/ppermute | solution.py:375
  65.9 16.7 %collective-permute-start.17 = (bf16[64,768]{1,0:T(8,128)(2,1)}, bf16[64,768]{1,0:T(8,128)(2,1)S(1)}, u32[]{:S(2)}, u32[]{:S(2)}) collective-permute-start(bf16[64,768]{1,0:T(8,128)(2,1)} %get-tuple-element.49), channel_id=1, source_target_pairs={{0,96},{16,176},{32,128},{48,208},{64,160},{80,240},{96,192},{112,... | collective-permute-start | bytes 294920 | tf_op jit(solution)/shard_map/ppermute | solution.py:375
  68.4 14.2 %collective-permute-start.18 = (bf16[64,768]{1,0:T(8,128)(2,1)}, bf16[64,768]{1,0:T(8,128)(2,1)S(1)}, u32[]{:S(2)}, u32[]{:S(2)}) collective-permute-start(bf16[64,768]{1,0:T(8,128)(2,1)} %get-tuple-element.50), channel_id=1, source_target_pairs={{0,160},{16,112},{32,192},{48,144},{64,224},{80,176},{96,0},{112,2... | collective-permute-start | bytes 294920 | tf_op jit(solution)/shard_map/ppermute | solution.py:375
  71.0 11.6 %collective-permute-start.20 = (bf16[64,768]{1,0:T(8,128)(2,1)}, bf16[64,768]{1,0:T(8,128)(2,1)S(1)}, u32[]{:S(2)}, u32[]{:S(2)}) collective-permute-start(bf16[64,768]{1,0:T(8,128)(2,1)} %get-tuple-element.52), channel_id=1, source_target_pairs={{0,32},{16,240},{32,64},{48,16},{64,96},{80,48},{96,128},{112,80},... | collective-permute-start | bytes 294920 | tf_op jit(solution)/shard_map/ppermute | solution.py:375
  73.5 13.2 %collective-permute-start.21 = (bf16[64,768]{1,0:T(8,128)(2,1)}, bf16[64,768]{1,0:T(8,128)(2,1)S(1)}, u32[]{:S(2)}, u32[]{:S(2)}) collective-permute-start(bf16[64,768]{1,0:T(8,128)(2,1)} %get-tuple-element.53), channel_id=1, source_target_pairs={{0,64},{16,208},{32,96},{48,240},{64,128},{80,16},{96,160},{112,48... | collective-permute-start | bytes 294920 | tf_op jit(solution)/shard_map/ppermute | solution.py:375
  75.0 12.4 %copy-start.41 = (bf16[64,768]{1,0:T(8,128)(2,1)}, bf16[64,768]{1,0:T(8,128)(2,1)S(1)}, u32[]{:S(2)}) copy-start(bf16[64,768]{1,0:T(8,128)(2,1)S(1)} %collective-permute-done.16.refs_0_.refs_4_) | copy-start | bytes 294916
  75.0 11.7 %collective-permute-start.22 = (bf16[64,768]{1,0:T(8,128)(2,1)}, bf16[64,768]{1,0:T(8,128)(2,1)S(1)}, u32[]{:S(2)}, u32[]{:S(2)}) collective-permute-start(bf16[64,768]{1,0:T(8,128)(2,1)} %get-tuple-element.54), channel_id=1, source_target_pairs={{0,192},{16,80},{32,224},{48,112},{64,0},{80,144},{96,32},{112,176... | collective-permute-start | bytes 294920 | tf_op jit(solution)/shard_map/ppermute | solution.py:375
  82.6 4.8 %copy-start.42 = (bf16[64,768]{1,0:T(8,128)(2,1)}, bf16[64,768]{1,0:T(8,128)(2,1)S(1)}, u32[]{:S(2)}) copy-start(bf16[64,768]{1,0:T(8,128)(2,1)S(1)} %collective-permute-done.17.refs_1_.refs_3_) | copy-start | bytes 294916
  82.6 4.8 %collective-permute-start.23 = (bf16[64,768]{1,0:T(8,128)(2,1)}, bf16[64,768]{1,0:T(8,128)(2,1)S(1)}, u32[]{:S(2)}, u32[]{:S(2)}) collective-permute-start(bf16[64,768]{1,0:T(8,128)(2,1)} %get-tuple-element.55), channel_id=1, source_target_pairs={{0,224},{16,48},{32,0},{48,80},{64,32},{80,112},{96,64},{112,144},... | collective-permute-start | bytes 294920 | tf_op jit(solution)/shard_map/ppermute | solution.py:375
  82.6 4.8 %copy-start.43 = (bf16[64,768]{1,0:T(8,128)(2,1)}, bf16[64,768]{1,0:T(8,128)(2,1)S(1)}, u32[]{:S(2)}) copy-start(bf16[64,768]{1,0:T(8,128)(2,1)S(1)} %collective-permute-done.18.refs_2_.refs_5_) | copy-start | bytes 294916
  82.6 4.8 %copy-start.44 = (bf16[64,768]{1,0:T(8,128)(2,1)}, bf16[64,768]{1,0:T(8,128)(2,1)S(1)}, u32[]{:S(2)}) copy-start(bf16[64,768]{1,0:T(8,128)(2,1)S(1)} %collective-permute-done.20.refs_1_) | copy-start | bytes 294916
  90.2 4.1 %copy-start.22 = (f32[8,128]{1,0:T(8,128)S(1)}, f32[8,128]{1,0:T(8,128)}, u32[]{:S(2)}) copy-start(f32[8,128]{1,0:T(8,128)} %get-tuple-element.56._) | copy-start | bytes 12292
  90.2 21.9 %collective-permute-start.24 = (bf16[8,64,768]{2,1,0:T(8,128)(2,1)}, bf16[8,64,768]{2,1,0:T(8,128)(2,1)S(1)}, u32[]{:S(2)}, u32[]{:S(2)}) collective-permute-start(bf16[8,64,768]{2,1,0:T(8,128)(2,1)} %get-tuple-element.59.refs_16_), channel_id=1, source_target_pairs={{0,1},{1,0},{2,3},{3,2},{4,5},{5,4},{6,7},{7,6},{8,9},{9,8},{10,11... | collective-permute-start | bytes 2359304 | tf_op jit(solution)/shard_map/ppermute | solution.py:384
  93.6 0.7 collective-permute-start.19
  95.7 16.4 %copy-start.4 = (bf16[64,1536]{1,0:T(8,128)(2,1)S(1)}, bf16[64,1536]{1,0:T(8,128)(2,1)}, u32[]{:S(2)}) copy-start(bf16[64,1536]{1,0:T(8,128)(2,1)} %copy-done.3) | copy-start | bytes 589828
  95.7 16.4 %copy-start.6 = (bf16[64,1536]{1,0:T(8,128)(2,1)S(1)}, bf16[64,1536]{1,0:T(8,128)(2,1)}, u32[]{:S(2)}) copy-start(bf16[64,1536]{1,0:T(8,128)(2,1)} %copy-done.5) | copy-start | bytes 589828
  95.7 16.4 %copy-start.8 = (bf16[64,1536]{1,0:T(8,128)(2,1)S(1)}, bf16[64,1536]{1,0:T(8,128)(2,1)}, u32[]{:S(2)}) copy-start(bf16[64,1536]{1,0:T(8,128)(2,1)} %copy-done.7) | copy-start | bytes 589828
  95.7 16.4 %copy-start.10 = (bf16[64,1536]{1,0:T(8,128)(2,1)S(1)}, bf16[64,1536]{1,0:T(8,128)(2,1)}, u32[]{:S(2)}) copy-start(bf16[64,1536]{1,0:T(8,128)(2,1)} %copy-done.9) | copy-start | bytes 589828
  95.7 16.4 %copy-start.12 = (bf16[64,1536]{1,0:T(8,128)(2,1)S(1)}, bf16[64,1536]{1,0:T(8,128)(2,1)}, u32[]{:S(2)}) copy-start(bf16[64,1536]{1,0:T(8,128)(2,1)} %copy-done.11) | copy-start | bytes 589828
  95.7 16.4 %copy-start.14 = (bf16[64,1536]{1,0:T(8,128)(2,1)S(1)}, bf16[64,1536]{1,0:T(8,128)(2,1)}, u32[]{:S(2)}) copy-start(bf16[64,1536]{1,0:T(8,128)(2,1)} %copy-done.13) | copy-start | bytes 589828
  95.7 16.4 %copy-start.16 = (bf16[64,1536]{1,0:T(8,128)(2,1)S(1)}, bf16[64,1536]{1,0:T(8,128)(2,1)}, u32[]{:S(2)}) copy-start(bf16[64,1536]{1,0:T(8,128)(2,1)} %copy-done.15) | copy-start | bytes 589828
  95.7 16.4 %copy-start.18 = (bf16[64,1536]{1,0:T(8,128)(2,1)S(1)}, bf16[64,1536]{1,0:T(8,128)(2,1)}, u32[]{:S(2)}) copy-start(bf16[64,1536]{1,0:T(8,128)(2,1)} %copy-done.17) | copy-start | bytes 589828
  95.7 16.4 %copy-start.20 = (s32[3]{0:T(128)S(1)}, s32[3]{0:T(128)}, u32[]{:S(2)}) copy-start(s32[3]{0:T(128)} %pad_add_fusion.refs_0_.at_ref) | copy-start | bytes 40
  95.7 16.4 %copy-start.23 = (bf16[8,64,768]{2,1,0:T(8,128)(2,1)S(1)}, bf16[8,64,768]{2,1,0:T(8,128)(2,1)}, u32[]{:S(2)}) copy-start(bf16[8,64,768]{2,1,0:T(8,128)(2,1)} %get-tuple-element.59.refs_16_) | copy-start | bytes 2359300
  95.7 16.4 %copy-start.25 = (bf16[64,1536]{1,0:T(8,128)(2,1)S(1)}, bf16[64,1536]{1,0:T(8,128)(2,1)}, u32[]{:S(2)}) copy-start(bf16[64,1536]{1,0:T(8,128)(2,1)} %get-tuple-element.34.first_ref.refs_1_.refs_0_) | copy-start | bytes 589828
  95.8 16.4 %copy-start.27 = (bf16[64,1536]{1,0:T(8,128)(2,1)S(1)}, bf16[64,1536]{1,0:T(8,128)(2,1)}, u32[]{:S(2)}) copy-start(bf16[64,1536]{1,0:T(8,128)(2,1)} %get-tuple-element.35.second_ref.refs_2_.refs_1_) | copy-start | bytes 589828
  95.8 42.2 %all-to-all-start.1 = ((bf16[16,64,896]{2,1,0:T(8,128)(2,1)}), bf16[16,64,896]{2,1,0:T(8,128)(2,1)}, u32[]{:S(2)}, u32[]{:S(2)}) async-start(bf16[16,64,896]{2,1,0:T(8,128)(2,1)} %get-tuple-element.57), calls=%async_computation.1 | async-start | bytes 3670016 | tf_op jit(solution)/shard_map/all_to_all | solution.py:392
  121.3 1.1 copy-start.2
  122.3 3.1 %collective-permute-start.25 = (bf16[384,1536]{1,0:T(8,128)(2,1)}, bf16[384,1536]{1,0:T(8,128)(2,1)S(1)}, u32[]{:S(2)}, u32[]{:S(2)}) collective-permute-start(bf16[384,1536]{1,0:T(8,128)(2,1)} %get-tuple-element.61), channel_id=1, source_target_pairs={{0,16},{16,0},{32,48},{48,32},{64,80},{80,64},{96,112},{112,96},{1... | collective-permute-start | bytes 3538952 | tf_op jit(solution)/shard_map/ppermute | solution.py:404
  125.4 12.6 %copy-start.40 = (bf16[384,1536]{1,0:T(8,128)(2,1)}, bf16[384,1536]{1,0:T(8,128)(2,1)S(1)}, u32[]{:S(2)}) copy-start(bf16[384,1536]{1,0:T(8,128)(2,1)S(1)} %collective-permute-done.25.come_hbm) | copy-start | bytes 3538948
  (13 other events, 10.8 us)
